TPU v7x, 1024 devices: a whole 4x4x32 slice. The times are simulated.
1024 devices in a mesh: bx: 16 (over y, x), by: 64 (over z, core).
Axes of the slice: x: 4, y: 4, z: 32, core: 2. Of those that a mesh axis runs over, the one named last changes fastest.
Arguments:
- populations: float32 [19, 128, 65536], P(None, 'bx', 'by')
- cover_codes: int32 [2, 128, 65536], P(None, 'bx', 'by'), may hold values from 0 to 9215, as said below
- sphere_cell: int32 [3, 16, 64, 4], P(None, 'bx', 'by'), may hold values from 0 to 63, as said below
- sphere_velocity: float32 [3, 16, 64, 4], P(None, 'bx', 'by'), may hold values from -0.08 to 0.08
- sphere_spin: float32 [3, 16, 64, 4], P(None, 'bx', 'by'), may hold values from -0.01 to 0.01
- relax_rates: float32 [15], replicated, may hold values from 0.7 to 1.9
Outputs:
- populations_next: float32 [19, 128, 65536], P(None, 'bx', 'by')
- sphere_load: float32 [6, 16, 64, 4], P(None, 'bx', 'by')
Inputs may be any that keep to these rules, and one draw needn't show every extreme that they name: `sphere_cell`: centres lie in their block, with z in [8, 56). `cover_codes`: the slot of a layer with a nonzero level names a sphere whose centre is within 9 cells of the cell; the two layers of a cell name different slots and their levels sum to 255 or less; slot is below 36.
All inputs are finite; a program needn't handle non-finite values.
Results may differ from a plain program's by a relative error of at most 0.0003.
Values sent between devices are 32-bit elements; how exact they have to be, the bound alone decides.
A program may use at most 32 MiB of HBM per device.

v0:
```python
import jax
import jax.numpy as jnp
import numpy as np
from jax import lax
from jax.sharding import PartitionSpec as P

NZ = 64
RADIUS = 8


VELOCITIES = np.array(
    [
        [0, 0, 0],
        [1, 0, 0],
        [-1, 0, 0],
        [0, 1, 0],
        [0, -1, 0],
        [0, 0, 1],
        [0, 0, -1],
        [1, 1, 0],
        [-1, -1, 0],
        [1, -1, 0],
        [-1, 1, 0],
        [1, 0, 1],
        [-1, 0, -1],
        [1, 0, -1],
        [-1, 0, 1],
        [0, 1, 1],
        [0, -1, -1],
        [0, 1, -1],
        [0, -1, 1],
    ]
)
WEIGHTS = np.array([1.0 / 3.0] + [1.0 / 18.0] * 6 + [1.0 / 36.0] * 12)
OPPOSITE = [0, 2, 1, 4, 3, 6, 5, 8, 7, 10, 9, 12, 11, 14, 13, 16, 15, 18, 17]
FRACTION_LEVELS = 255.0


def padded(value, sides, width):
    for axis, dim in sides:
        devices, length = (lax.axis_size(axis), value.shape[dim])
        up = [(i, (i + 1) % devices) for i in range(devices)]
        down = [(j, i) for i, j in up]
        last = lax.slice_in_dim(value, length - width, length, axis=dim)
        first = lax.slice_in_dim(value, 0, width, axis=dim)
        before = lax.ppermute(last, axis, up)
        after = lax.ppermute(first, axis, down)
        value = jnp.concatenate([before, value, after], axis=dim)
    return value


def moment_rows():
    vel_x, vel_y, vel_z = [VELOCITIES[:, component] * 1.0 for component in range(3)]
    monomials = [
        np.ones(19),
        vel_x,
        vel_y,
        vel_z,
        vel_x * vel_x,
        vel_y * vel_y,
        vel_z * vel_z,
        vel_x * vel_y,
        vel_x * vel_z,
        vel_y * vel_z,
        vel_x * vel_x * vel_y,
        vel_x * vel_x * vel_z,
        vel_y * vel_y * vel_x,
        vel_y * vel_y * vel_z,
        vel_z * vel_z * vel_x,
        vel_z * vel_z * vel_y,
        vel_x * vel_x * vel_y * vel_y,
        vel_x * vel_x * vel_z * vel_z,
        vel_y * vel_y * vel_z * vel_z,
    ]
    orthonormal = []
    for vector in monomials:
        vector = vector.copy()
        for earlier in orthonormal:
            vector = vector - np.dot(earlier, vector) * earlier
        orthonormal.append(vector / np.sqrt(np.dot(vector, vector)))
    return np.stack(orthonormal)


def collision_matrix(relax_rates):
    moments = jnp.asarray(moment_rows(), jnp.float32)
    rate_full = jnp.concatenate([jnp.zeros((4,), jnp.float32), relax_rates])
    return jnp.dot(moments.T * rate_full[None, :], moments, precision=lax.Precision.HIGHEST)


def equilibrium(density, vel_x, vel_y, vel_z):
    square = vel_x * vel_x + vel_y * vel_y + vel_z * vel_z
    pieces = []
    for pop_index in range(19):
        aligned = (
            float(VELOCITIES[pop_index, 0]) * vel_x
            + float(VELOCITIES[pop_index, 1]) * vel_y
            + float(VELOCITIES[pop_index, 2]) * vel_z
        )
        pieces.append(
            float(WEIGHTS[pop_index])
            * density
            * (1.0 + 3.0 * aligned + 4.5 * aligned * aligned - 1.5 * square)
        )
    return jnp.stack(pieces)


def project_on(values, component):
    running = jnp.zeros(values.shape[1:], jnp.float32)
    for pop_index in range(19):
        factor = int(VELOCITIES[pop_index, component])
        if factor != 0:
            running = running + float(factor) * values[pop_index]
    return running


def collide_block(populations, cover_codes, slot_rows, relax_rates):
    width_x = populations.shape[1]
    flat_cells = populations.shape[2]
    width_y = flat_cells // NZ
    slots = slot_rows.shape[0]
    per_block = slots // 9
    slot_ids = jnp.arange(slots, dtype=jnp.int32)
    shift_x = (slot_ids // (3 * per_block) - 1).astype(jnp.float32) * float(width_x)
    shift_y = (slot_ids // per_block % 3 - 1).astype(jnp.float32) * float(width_y)
    columns = [slot_rows[:, 0] + shift_x, slot_rows[:, 1] + shift_y] + [
        slot_rows[:, component] for component in range(2, 9)
    ]
    slot_table = jnp.stack(columns)
    flat_ids = jnp.arange(flat_cells, dtype=jnp.int32)
    cell_x = jnp.broadcast_to(
        jnp.arange(width_x, dtype=jnp.int32).astype(jnp.float32)[:, None], (width_x, flat_cells)
    )
    cell_y = jnp.broadcast_to((flat_ids // NZ).astype(jnp.float32)[None, :], (width_x, flat_cells))
    cell_z = jnp.broadcast_to((flat_ids % NZ).astype(jnp.float32)[None, :], (width_x, flat_cells))
    density = jnp.sum(populations, axis=0)
    flow_x = project_on(populations, 0) / density
    flow_y = project_on(populations, 1) / density
    flow_z = project_on(populations, 2) / density
    balance = equilibrium(density, flow_x, flow_y, flow_z)
    relax_matrix = collision_matrix(relax_rates)
    fluid_term = -jnp.einsum(
        "ij,jxc->ixc", relax_matrix, populations - balance, precision=lax.Precision.HIGHEST
    )
    collided = populations + fluid_term
    mirror = jnp.stack([populations[other] - balance[other] for other in OPPOSITE])
    slot_loads = jnp.zeros((slots, 6), jnp.float32)
    radius_two = float(RADIUS * RADIUS)
    radius_three = float(RADIUS * RADIUS * RADIUS)
    for cover_layer in range(2):
        packed = cover_codes[cover_layer]
        slot_of = packed // 256
        fraction = (packed % 256).astype(jnp.float32) / FRACTION_LEVELS
        onehot = (slot_of[None, :, :] == slot_ids[:, None, None]).astype(jnp.float32)
        values = jnp.einsum("ks,sxc->kxc", slot_table, onehot, precision=lax.Precision.HIGHEST)
        rel_x = cell_x - values[0]
        rel_y = cell_y - values[1]
        rel_z = cell_z - values[2]
        wall_x = values[3] + values[7] * rel_z - values[8] * rel_y
        wall_y = values[4] + values[8] * rel_x - values[6] * rel_z
        wall_z = values[5] + values[6] * rel_y - values[7] * rel_x
        solid_term = mirror + equilibrium(density, wall_x, wall_y, wall_z) - populations
        collided = collided + fraction[None] * (solid_term - fluid_term)
        force_x = -fraction * project_on(solid_term, 0)
        force_y = -fraction * project_on(solid_term, 1)
        force_z = -fraction * project_on(solid_term, 2)
        torque_x = rel_y * force_z - rel_z * force_y
        torque_y = rel_z * force_x - rel_x * force_z
        torque_z = rel_x * force_y - rel_y * force_x
        contrib = jnp.stack(
            [
                force_x / radius_two,
                force_y / radius_two,
                force_z / radius_two,
                torque_x / radius_three,
                torque_y / radius_three,
                torque_z / radius_three,
            ]
        )
        slot_loads = slot_loads + jnp.einsum(
            "sxc,kxc->sk", onehot, contrib, precision=lax.Precision.HIGHEST
        )
    return (collided, slot_loads)


def along_z(shifted, bounce, offset_z):
    if offset_z == 1:
        return jnp.concatenate([bounce[..., :1], shifted[..., :-1]], axis=-1)
    if offset_z == -1:
        return jnp.concatenate([shifted[..., 1:], bounce[..., -1:]], axis=-1)
    return shifted


def per_device(populations, cover_codes, sphere_cell, sphere_velocity, sphere_spin, relax_rates):
    pop_total, width_x, flat_cells = populations.shape
    width_y = flat_cells // NZ
    per_block = sphere_cell.shape[3]
    own_rows = jnp.concatenate(
        [sphere_cell.astype(jnp.float32), sphere_velocity, sphere_spin], axis=0
    ).transpose(1, 2, 0, 3)
    neighbours = padded(own_rows, (("bx", 0), ("by", 1)), 1)
    slot_rows = neighbours.transpose(0, 1, 3, 2).reshape(9 * per_block, 9)
    collided, slot_loads = collide_block(populations, cover_codes, slot_rows, relax_rates)
    grid = collided.reshape(pop_total, width_x, width_y, NZ)
    shifted_of = []
    widened = padded(grid, (("bx", 1), ("by", 2)), 1)
    for pop_index in range(19):
        step_x = int(VELOCITIES[pop_index, 0])
        step_y = int(VELOCITIES[pop_index, 1])
        shifted_of.append(
            widened[pop_index, 1 - step_x : 1 - step_x + width_x, 1 - step_y : 1 - step_y + width_y]
        )
    passed = []
    for pop_index in range(19):
        passed.append(
            along_z(shifted_of[pop_index], grid[OPPOSITE[pop_index]], int(VELOCITIES[pop_index, 2]))
        )
    populations_next = jnp.stack(passed).reshape(pop_total, width_x, flat_cells)
    slot_parts = slot_loads.reshape(3, 3, per_block * 6)
    widened_loads = padded(slot_parts, (("bx", 0), ("by", 1)), 1)
    owned_load = jnp.zeros((per_block * 6,), jnp.float32)
    for edge_x in (0, 2, 4):
        for edge_y in (0, 2, 4):
            owned_load = owned_load + widened_loads[edge_x, edge_y]
    sphere_load = owned_load.reshape(per_block, 6).T[:, None, None, :]
    return (populations_next, sphere_load)


def solution(mesh):
    placed = (
        P(None, "bx", "by"),
        P(None, "bx", "by"),
        P(None, "bx", "by", None),
        P(None, "bx", "by", None),
        P(None, "bx", "by", None),
        P(),
    )
    return jax.shard_map(
        per_device,
        mesh=mesh,
        in_specs=placed,
        out_specs=(P(None, "bx", "by"), P(None, "bx", "by", None)),
        check_vma=False,
    )
```

profile of v0, /device:TPU:1, one launch (start us, length us, event | category | flops | bytes accessed | tf_op | source)
XLA Modules:
  0.0 85.7 jit_solution(18276672028354620753)
XLA Ops:
  0.7 0.7 copy_convert_fusion
  1.4 0.1 copy.145
  1.5 0.8 copy.146
  2.3 0.8 copy.147
  3.1 3.9 %collective-permute-start = (f32[1,1,9,4]{2,3,1,0:T(4,128)S(1)}, f32[1,1,9,4]{2,3,1,0:T(4,128)S(1)}, u32[]{:S(2)}, u32[]{:S(2)}) collective-permute-start(f32[1,1,9,4]{2,3,1,0:T(4,128)S(1)} %maximum_bitcast_fusion.3), channel_id=1, source_target_pairs={{0,64},{64,128},{128,192},{192,256},{256,320},{320,384},{384,448},... | collective-permute-start | bytes 440 | tf_op jit(solution)/shard_map/ppermute | solution.py:46
  7.1 5.6 %collective-permute-start.1 = (f32[1,1,9,4]{2,3,1,0:T(4,128)S(1)}, f32[1,1,9,4]{2,3,1,0:T(4,128)S(1)}, u32[]{:S(2)}, u32[]{:S(2)}) collective-permute-start(f32[1,1,9,4]{2,3,1,0:T(4,128)S(1)} %maximum_bitcast_fusion.3), channel_id=1, source_target_pairs={{64,0},{128,64},{192,128},{256,192},{320,256},{384,320},{448,384},... | collective-permute-start | bytes 440 | tf_op jit(solution)/shard_map/ppermute | solution.py:47
  12.7 0.8 fusion.287
  13.5 1.1 %reduce_sum.11 = f32[8,1024]{1,0:T(8,128)S(1)} reduce(f32[19,8,1024]{2,1,0:T(8,128)} %param.7, f32[]{:T(128)} %constant.122.clone.1), dimensions={0}, to_apply=%region_0.1 | reduce | flops 147456 | bytes 655364 | tf_op jit(solution)/shard_map/reduce_sum | solution.py:135
  14.7 1.1 %constant_dynamic-update-slice_fusion.18 = (f32[19,8,1024]{2,1,0:T(8,128)S(1)}, f32[1,8,1024]{2,1,0:T(8,128)S(1)}, f32[1,8,1024]{2,1,0:T(8,128)S(1)}, f32[1,8,10...) fusion(f32[8,1024]{1,0:T(8,128)S(1)} %reduce_sum.11, f32[19,8,1024]{2,1,0:T(8,128)} %param.7), kind=kLoop, calls=%fused_computation.40 | loop fusion | flops 499711 | bytes 819200
  16.0 0.3 convolution_bitcast_fusion
  16.3 2.6 %collective-permute-start.2 = (f32[3,1,9,4]{2,3,1,0:T(4,128)S(1)}, f32[3,1,9,4]{2,3,1,0:T(4,128)S(1)}, u32[]{:S(2)}, u32[]{:S(2)}) collective-permute-start(f32[3,1,9,4]{2,3,1,0:T(4,128)S(1)} %pad_maximum_fusion.18), channel_id=1, source_target_pairs={{0,1},{1,2},{2,3},{3,4},{4,5},{5,6},{6,7},{7,8},{8,9},{9,10},{10,1... | collective-permute-start | bytes 1304 | tf_op jit(solution)/shard_map/ppermute | solution.py:46
  18.9 11.2 %collective-permute-start.3 = (f32[3,1,9,4]{2,3,1,0:T(4,128)S(1)}, f32[3,1,9,4]{2,3,1,0:T(4,128)S(1)}, u32[]{:S(2)}, u32[]{:S(2)}) collective-permute-start(f32[3,1,9,4]{2,3,1,0:T(4,128)S(1)} %pad_maximum_fusion.18), channel_id=1, source_target_pairs={{1,0},{2,1},{3,2},{4,3},{5,4},{6,5},{7,6},{8,7},{9,8},{10,9},{11,1... | collective-permute-start | bytes 1304 | tf_op jit(solution)/shard_map/ppermute | solution.py:47
  30.0 0.6 collective-permute-done.2
  30.7 0.2 collective-permute-done.3
  30.9 0.3 slice_reduce_fusion
  31.3 0.5 fusion.1
  31.9 0.2 fusion.322
  32.1 0.1 constant_dynamic-update-slice_fusion.75
  32.6 0.5 fusion.3
  33.1 0.2 fusion.323
  33.3 0.1 constant_dynamic-update-slice_fusion.56
  34.8 1.1 %fusion.7 = f32[19,8,1024]{2,0,1:T(8,128)S(1)} fusion(f32[19,19,1]{1,0,2:T(8,128)S(1)} %convolution_bitcast_fusion, f32[19,8,1024]{2,1,0:T(8,128)S(1)} %sub.691), kind=kOutput, calls=%fused_computation.10 | convolution fusion | flops 35487744 | bytes 1246628 | tf_op jit(solution)/shard_map/ij,jxc->ixc/dot_general | solution.py:141
  35.9 0.7 multiply_add_fusion
  37.1 0.8 fusion.4
  37.8 0.8 fusion.6
  38.7 0.1 copy.169
  38.8 0.3 reshape.1118
  39.1 0.6 fusion.321
  39.8 0.1 copy.168
  40.0 1.9 %collective-permute-start.8 = (f32[1,3,24]{2,1,0:T(4,128)S(1)}, f32[1,3,24]{2,1,0:T(4,128)S(1)}, u32[]{:S(2)}, u32[]{:S(2)}) collective-permute-start(f32[1,3,24]{2,1,0:T(4,128)S(1)} %slice.675), channel_id=1, source_target_pairs={{0,64},{64,128},{128,192},{192,256},{256,320},{320,384},{384,448},... | collective-permute-start | bytes 872 | tf_op jit(solution)/shard_map/ppermute | solution.py:46
  42.0 0.1 copy.170
  42.1 6.7 %collective-permute-start.9 = (f32[1,3,24]{2,1,0:T(4,128)S(1)}, f32[1,3,24]{2,1,0:T(4,128)S(1)}, u32[]{:S(2)}, u32[]{:S(2)}) collective-permute-start(f32[1,3,24]{2,1,0:T(4,128)S(1)} %slice.677), channel_id=1, source_target_pairs={{64,0},{128,64},{192,128},{256,192},{320,256},{384,320},{448,384},... | collective-permute-start | bytes 872 | tf_op jit(solution)/shard_map/ppermute | solution.py:47
  48.8 1.9 %collective-permute-start.4 = (f32[19,1,16,64]{3,2,1,0:T(8,128)S(1)}, f32[19,1,16,64]{3,2,1,0:T(8,128)}, u32[]{:S(2)}, u32[]{:S(2)}) collective-permute-start(f32[19,1,16,64]{3,2,1,0:T(8,128)S(1)} %get-tuple-element.112), channel_id=1, source_target_pairs={{0,64},{64,128},{128,192},{192,256},{256,320},{320,384},{384,448},... | collective-permute-start | bytes 233480 | tf_op jit(solution)/shard_map/ppermute | solution.py:46
  50.8 6.7 %collective-permute-start.5 = (f32[19,1,16,64]{3,2,1,0:T(8,128)S(1)}, f32[19,1,16,64]{3,2,1,0:T(8,128)}, u32[]{:S(2)}, u32[]{:S(2)}) collective-permute-start(f32[19,1,16,64]{3,2,1,0:T(8,128)S(1)} %get-tuple-element.111), channel_id=1, source_target_pairs={{64,0},{128,64},{192,128},{256,192},{320,256},{384,320},{448,384},... | collective-permute-start | bytes 233480 | tf_op jit(solution)/shard_map/ppermute | solution.py:47
  58.2 0.1 pad_maximum_fusion.9
  58.7 4.8 %collective-permute-start.11 = (f32[5,1,24]{2,1,0:T(1,128)S(1)}, f32[5,1,24]{2,1,0:T(1,128)S(1)}, u32[]{:S(2)}, u32[]{:S(2)}) collective-permute-start(f32[5,1,24]{2,1,0:T(1,128)S(1)} %get-tuple-element.163), channel_id=1, source_target_pairs={{1,0},{2,1},{3,2},{4,3},{5,4},{6,5},{7,6},{8,7},{9,8},{10,9},{11,1... | collective-permute-start | bytes 1448 | tf_op jit(solution)/shard_map/ppermute | solution.py:47
  64.0 0.1 collective-permute-done.10
  64.1 0.2 collective-permute-done.11
  64.4 0.7 reshape.1123
  65.0 0.9 %constant_dynamic-update-slice_fusion.82 = (f32[19,10,16,64]{3,2,1,0:T(8,128)S(1)}, f32[19,9,16,64]{3,2,1,0:T(8,128)S(1)}) fusion(f32[19,1,16,64]{3,2,1,0:T(8,128)} %collective-permute-done.4), kind=kLoop, calls=%fused_computation.104 | loop fusion | bytes 389120
  66.0 0.4 constant_dynamic-update-slice_fusion.81
  66.3 0.9 %constant_dynamic-update-slice_fusion.80 = (f32[19,10,16,64]{3,2,1,0:T(8,128)S(1)}, f32[19,9,16,64]{3,2,1,0:T(8,128)S(1)}) fusion(f32[19,10,16,64]{3,2,1,0:T(8,128)S(1)} %get-tuple-element.108, f32[19,1,16,64]{3,2,1,0:T(8,128)} %collective-permute-done.5, f32[19,9,16,64]{3,2,1,0:T(8,128)S(1)} %get-tuple-element.109), kind=kLoop, calls=%fused_computation.102 | loop fusion | bytes 389120 | tf_op jit(solution)/shard_map/concatenate | solution.py:48
  67.3 0.1 fusion.319
  67.4 3.4 %collective-permute-start.7 = (f32[19,10,1,64]{3,2,1,0:T(1,128)S(1)}, f32[19,10,1,64]{3,2,1,0:T(1,128)S(1)}, u32[]{:S(2)}, u32[]{:S(2)}) collective-permute-start(f32[19,10,1,64]{3,2,1,0:T(1,128)S(1)} %get-tuple-element.100), channel_id=1, source_target_pairs={{1,0},{2,1},{3,2},{4,3},{5,4},{6,5},{7,6},{8,7},{9,8},{10,9},{11,1... | collective-permute-start | bytes 145928 | tf_op jit(solution)/shard_map/ppermute | solution.py:47
  71.1 0.1 stack.58
  71.6 0.6 constant_dynamic-update-slice_fusion.100
  72.2 0.6 constant_dynamic-update-slice_fusion.99
  73.4 1.1 %collective-permute-done.6 = f32[19,10,1,64]{3,2,1,0:T(1,128)S(1)} collective-permute-done((f32[19,10,1,64]{3,2,1,0:T(1,128)S(1)}, f32[19,10,1,64]{3,2,1,0:T(1,128)S(1)}, u32[]{:S(2)}, u32[]{:S(2)}) %collective-permute-start.6) | collective-permute-done | bytes 48672 | tf_op jit(solution)/shard_map/ppermute | solution.py:46
  75.8 0.6 constant_dynamic-update-slice_fusion.98
  76.4 0.6 constant_dynamic-update-slice_fusion.97
  77.1 0.6 constant_dynamic-update-slice_fusion.96
  77.7 0.6 constant_dynamic-update-slice_fusion.95
  78.3 0.6 constant_dynamic-update-slice_fusion.94
  78.9 0.6 constant_dynamic-update-slice_fusion.93
  79.5 0.6 constant_dynamic-update-slice_fusion.92
  80.1 0.6 constant_dynamic-update-slice_fusion.91
  80.8 0.6 constant_dynamic-update-slice_fusion.90
  81.4 0.6 constant_dynamic-update-slice_fusion.89
  82.0 0.6 constant_dynamic-update-slice_fusion.88
  82.6 0.6 constant_dynamic-update-slice_fusion.87
  83.2 0.6 constant_dynamic-update-slice_fusion.86
  83.8 0.6 constant_dynamic-update-slice_fusion.85
  84.5 0.6 constant_dynamic-update-slice_fusion.84
  85.1 0.6 constant_dynamic-update-slice_fusion.83
  (162 shorter events, 6.5 us)
Async XLA Ops:
  0.6 15.3 %copy-start.3 = (f32[19,19]{1,0:T(8,128)S(1)}, f32[19,19]{1,0:T(8,128)}, u32[]{:S(2)}) copy-start(f32[19,19]{1,0:T(8,128)} %constant.148.clone) | copy-start | bytes 4336
  0.6 15.2 %copy-start.1 = (s32[2,8,1024]{2,1,0:T(8,128)S(1)}, s32[2,8,1024]{2,1,0:T(8,128)}, u32[]{:S(2)}) copy-start(s32[2,8,1024]{2,1,0:T(8,128)} %param.8) | copy-start | bytes 196612
  0.7 15.1 %copy-start = (f32[19,8,1024]{2,1,0:T(8,128)S(1)}, f32[19,8,1024]{2,1,0:T(8,128)}, u32[]{:S(2)}) copy-start(f32[19,8,1024]{2,1,0:T(8,128)} %param.7) | copy-start | bytes 1867780
  0.7 15.1 %copy-start.2 = (f32[15]{0:T(128)S(1)}, f32[15]{0:T(128)}, u32[]{:S(2)}) copy-start(f32[15]{0:T(128)} %param.12) | copy-start | bytes 184
  3.1 13.1 %collective-permute-start = (f32[1,1,9,4]{2,3,1,0:T(4,128)S(1)}, f32[1,1,9,4]{2,3,1,0:T(4,128)S(1)}, u32[]{:S(2)}, u32[]{:S(2)}) collective-permute-start(f32[1,1,9,4]{2,3,1,0:T(4,128)S(1)} %maximum_bitcast_fusion.3), channel_id=1, source_target_pairs={{0,64},{64,128},{128,192},{192,256},{256,320},{320,384},{384,448},... | collective-permute-start | bytes 440 | tf_op jit(solution)/shard_map/ppermute | solution.py:46
  7.1 9.2 %collective-permute-start.1 = (f32[1,1,9,4]{2,3,1,0:T(4,128)S(1)}, f32[1,1,9,4]{2,3,1,0:T(4,128)S(1)}, u32[]{:S(2)}, u32[]{:S(2)}) collective-permute-start(f32[1,1,9,4]{2,3,1,0:T(4,128)S(1)} %maximum_bitcast_fusion.3), channel_id=1, source_target_pairs={{64,0},{128,64},{192,128},{256,192},{320,256},{384,320},{448,384},... | collective-permute-start | bytes 440 | tf_op jit(solution)/shard_map/ppermute | solution.py:47
  16.3 14.4 %collective-permute-start.2 = (f32[3,1,9,4]{2,3,1,0:T(4,128)S(1)}, f32[3,1,9,4]{2,3,1,0:T(4,128)S(1)}, u32[]{:S(2)}, u32[]{:S(2)}) collective-permute-start(f32[3,1,9,4]{2,3,1,0:T(4,128)S(1)} %pad_maximum_fusion.18), channel_id=1, source_target_pairs={{0,1},{1,2},{2,3},{3,4},{4,5},{5,6},{6,7},{7,8},{8,9},{9,10},{10,1... | collective-permute-start | bytes 1304 | tf_op jit(solution)/shard_map/ppermute | solution.py:46
  18.9 12.0 %collective-permute-start.3 = (f32[3,1,9,4]{2,3,1,0:T(4,128)S(1)}, f32[3,1,9,4]{2,3,1,0:T(4,128)S(1)}, u32[]{:S(2)}, u32[]{:S(2)}) collective-permute-start(f32[3,1,9,4]{2,3,1,0:T(4,128)S(1)} %pad_maximum_fusion.18), channel_id=1, source_target_pairs={{1,0},{2,1},{3,2},{4,3},{5,4},{6,5},{7,6},{8,7},{9,8},{10,9},{11,1... | collective-permute-start | bytes 1304 | tf_op jit(solution)/shard_map/ppermute | solution.py:47
  40.0 18.7 %collective-permute-start.8 = (f32[1,3,24]{2,1,0:T(4,128)S(1)}, f32[1,3,24]{2,1,0:T(4,128)S(1)}, u32[]{:S(2)}, u32[]{:S(2)}) collective-permute-start(f32[1,3,24]{2,1,0:T(4,128)S(1)} %slice.675), channel_id=1, source_target_pairs={{0,64},{64,128},{128,192},{192,256},{256,320},{320,384},{384,448},... | collective-permute-start | bytes 872 | tf_op jit(solution)/shard_map/ppermute | solution.py:46
  42.1 16.5 %collective-permute-start.9 = (f32[1,3,24]{2,1,0:T(4,128)S(1)}, f32[1,3,24]{2,1,0:T(4,128)S(1)}, u32[]{:S(2)}, u32[]{:S(2)}) collective-permute-start(f32[1,3,24]{2,1,0:T(4,128)S(1)} %slice.677), channel_id=1, source_target_pairs={{64,0},{128,64},{192,128},{256,192},{320,256},{384,320},{448,384},... | collective-permute-start | bytes 872 | tf_op jit(solution)/shard_map/ppermute | solution.py:47
  48.8 16.2 %collective-permute-start.4 = (f32[19,1,16,64]{3,2,1,0:T(8,128)S(1)}, f32[19,1,16,64]{3,2,1,0:T(8,128)}, u32[]{:S(2)}, u32[]{:S(2)}) collective-permute-start(f32[19,1,16,64]{3,2,1,0:T(8,128)S(1)} %get-tuple-element.112), channel_id=1, source_target_pairs={{0,64},{64,128},{128,192},{192,256},{256,320},{320,384},{384,448},... | collective-permute-start | bytes 233480 | tf_op jit(solution)/shard_map/ppermute | solution.py:46
  50.8 15.6 %collective-permute-start.5 = (f32[19,1,16,64]{3,2,1,0:T(8,128)S(1)}, f32[19,1,16,64]{3,2,1,0:T(8,128)}, u32[]{:S(2)}, u32[]{:S(2)}) collective-permute-start(f32[19,1,16,64]{3,2,1,0:T(8,128)S(1)} %get-tuple-element.111), channel_id=1, source_target_pairs={{64,0},{128,64},{192,128},{256,192},{320,256},{384,320},{448,384},... | collective-permute-start | bytes 233480 | tf_op jit(solution)/shard_map/ppermute | solution.py:47
  58.7 5.5 %collective-permute-start.10 = (f32[5,1,24]{2,1,0:T(1,128)S(1)}, f32[5,1,24]{2,1,0:T(1,128)S(1)}, u32[]{:S(2)}, u32[]{:S(2)}) collective-permute-start(f32[5,1,24]{2,1,0:T(1,128)S(1)} %get-tuple-element.162), channel_id=1, source_target_pairs={{0,1},{1,2},{2,3},{3,4},{4,5},{5,6},{6,7},{7,8},{8,9},{9,10},{10,1... | collective-permute-start | bytes 1448 | tf_op jit(solution)/shard_map/ppermute | solution.py:46
  58.7 5.6 %collective-permute-start.11 = (f32[5,1,24]{2,1,0:T(1,128)S(1)}, f32[5,1,24]{2,1,0:T(1,128)S(1)}, u32[]{:S(2)}, u32[]{:S(2)}) collective-permute-start(f32[5,1,24]{2,1,0:T(1,128)S(1)} %get-tuple-element.163), channel_id=1, source_target_pairs={{1,0},{2,1},{3,2},{4,3},{5,4},{6,5},{7,6},{8,7},{9,8},{10,9},{11,1... | collective-permute-start | bytes 1448 | tf_op jit(solution)/shard_map/ppermute | solution.py:47
  67.4 5.8 %collective-permute-start.7 = (f32[19,10,1,64]{3,2,1,0:T(1,128)S(1)}, f32[19,10,1,64]{3,2,1,0:T(1,128)S(1)}, u32[]{:S(2)}, u32[]{:S(2)}) collective-permute-start(f32[19,10,1,64]{3,2,1,0:T(1,128)S(1)} %get-tuple-element.100), channel_id=1, source_target_pairs={{1,0},{2,1},{3,2},{4,3},{5,4},{6,5},{7,6},{8,7},{9,8},{10,9},{11,1... | collective-permute-start | bytes 145928 | tf_op jit(solution)/shard_map/ppermute | solution.py:47
  70.9 3.7 %collective-permute-start.6 = (f32[19,10,1,64]{3,2,1,0:T(1,128)S(1)}, f32[19,10,1,64]{3,2,1,0:T(1,128)S(1)}, u32[]{:S(2)}, u32[]{:S(2)}) collective-permute-start(f32[19,10,1,64]{3,2,1,0:T(1,128)S(1)} %get-tuple-element.101), channel_id=1, source_target_pairs={{0,1},{1,2},{2,3},{3,4},{4,5},{5,6},{6,7},{7,8},{8,9},{9,10},{10,1... | collective-permute-start | bytes 145928 | tf_op jit(solution)/shard_map/ppermute | solution.py:46
where the time goes:
time: 86.3 us; the launch traced here: 85.7 us
  starting transfers between devices  48.8 us (57%)
  local copies, waits for them, and re-layouts  21.4 us (25%)
  other arithmetic  7.67 us (9%)
  matrix products  3.96 us (5%)
  waiting for transfers between devices  2.31 us (3%)
  between operations  1.57 us (2%)
    ppermute x6, starting transfers between devices, padded(): after = lax.ppermute(first, axis, down)  38.4 us
    unnamed x31, local copies, waits for them, and re-layouts  13.3 us
    ppermute x6, starting transfers between devices, padded(): before = lax.ppermute(last, axis, up)  10.4 us
    unnamed x74, other arithmetic  2.96 us
    another operation x19, local copies, waits for them, and re-layouts, per_device(): populations_next = jnp.stack(passed).reshape(pop_total, width_x, flat_cells)  2.12 us
    ppermute x6, waiting for transfers between devices, padded(): before = lax.ppermute(last, axis, up)  1.92 us
  transfers between devices with their start and end apart: 12, of which 5 were waited for; matrix products, arithmetic and copies ran while one was open for 12% of the time, Pallas kernels for 0%

commit v1 on v0

v1 whole, which is shorter than its diff:
```python
import jax
import jax.numpy as jnp
import numpy as np
from jax import lax
from jax.experimental import pallas as pl
from jax.experimental.pallas import tpu as pltpu
from jax.sharding import PartitionSpec as P

NZ = 64
RADIUS = 8
CX, CY = 8, 16
CELLS = CY * NZ
LANES = 128
CHUNKS = CELLS // LANES
MESH = pl.DeviceIdType.MESH
F32 = jnp.float32

VELOCITIES = np.array(
    [
        [0, 0, 0],
        [1, 0, 0],
        [-1, 0, 0],
        [0, 1, 0],
        [0, -1, 0],
        [0, 0, 1],
        [0, 0, -1],
        [1, 1, 0],
        [-1, -1, 0],
        [1, -1, 0],
        [-1, 1, 0],
        [1, 0, 1],
        [-1, 0, -1],
        [1, 0, -1],
        [-1, 0, 1],
        [0, 1, 1],
        [0, -1, -1],
        [0, 1, -1],
        [0, -1, 1],
    ]
)
OPPOSITE = [0, 2, 1, 4, 3, 6, 5, 8, 7, 10, 9, 12, 11, 14, 13, 16, 15, 18, 17]
X_UP, X_DOWN = (1, 7, 9, 11, 13), (2, 8, 10, 12, 14)
Y_UP, Y_DOWN = (3, 7, 10, 15, 17), (4, 8, 9, 16, 18)
DIRECTIONS = [d for d in range(9) if d != 4]


def moment_rows():
    vel_x, vel_y, vel_z = [VELOCITIES[:, component] * 1.0 for component in range(3)]
    monomials = [
        np.ones(19),
        vel_x,
        vel_y,
        vel_z,
        vel_x * vel_x,
        vel_y * vel_y,
        vel_z * vel_z,
        vel_x * vel_y,
        vel_x * vel_z,
        vel_y * vel_z,
        vel_x * vel_x * vel_y,
        vel_x * vel_x * vel_z,
        vel_y * vel_y * vel_x,
        vel_y * vel_y * vel_z,
        vel_z * vel_z * vel_x,
        vel_z * vel_z * vel_y,
        vel_x * vel_x * vel_y * vel_y,
        vel_x * vel_x * vel_z * vel_z,
        vel_y * vel_y * vel_z * vel_z,
    ]
    orthonormal = []
    for vector in monomials:
        vector = vector.copy()
        for earlier in orthonormal:
            vector = vector - np.dot(earlier, vector) * earlier
        orthonormal.append(vector / np.sqrt(np.dot(vector, vector)))
    return np.stack(orthonormal)


def coefficient_rows():
    rows = moment_rows()[4:]
    even = [1, 3, 5, 7, 11, 15]
    out = []
    for a in even:
        for b in even:
            keep = np.isin(np.arange(15), [0, 1, 2, 12, 13, 14])
            out.append(rows[:, a] * (rows[:, b] - rows[:, 0]) * keep)
    for axis, first, second, rates in ((1, 7, 11, (8, 10)), (3, 7, 15, (6, 11)), (5, 11, 15, (7, 9))):
        for a in (first, second):
            for b in (first, second):
                keep = np.isin(np.arange(15), rates)
                out.append(rows[:, a] * (rows[:, b] - rows[:, axis]) * keep)
    for rate in (3, 4, 5):
        out.append(0.25 * (np.arange(15) == rate))
    table = np.zeros((64, 16), np.float32)
    table[: len(out), :15] = np.stack(out)
    return table


def lane_shift(pop):
    return int(VELOCITIES[pop, 1]) * NZ + int(VELOCITIES[pop, 2])


def kernel(
    pops_hbm, codes_hbm, cell_ref, vel_ref, spin_ref, rates_ref, coef_in,
    out_hbm, load_ref,
    f, codes, coef, post, moments, onehot, contrib, split, out,
    state, states, table, xsend, xrecv, ysend, yrecv, loads, loads_in,
    in_sem, out_sem, state_send, state_recv, halo_send, halo_recv, load_send, load_recv,
):
    nx, ny = lax.axis_size("bx"), lax.axis_size("by")
    me_x, me_y = lax.axis_index("bx"), lax.axis_index("by")

    def neighbour(d):
        return (lax.rem(me_x + d // 3 - 1 + nx, nx), lax.rem(me_y + d % 3 - 1 + ny, ny))

    barrier = pltpu.get_barrier_semaphore()
    for d in DIRECTIONS:
        pl.semaphore_signal(barrier, inc=1, device_id=neighbour(d), device_id_type=MESH)
    get_codes = pltpu.make_async_copy(codes_hbm, codes, in_sem.at[0])
    get_codes.start()
    get_pops = pltpu.make_async_copy(pops_hbm, f, in_sem.at[1])
    get_pops.start()

    lane = lax.broadcasted_iota(jnp.int32, (1, LANES), 1)
    sphere = lane & 3
    for row in range(9):
        source = (cell_ref, vel_ref, spin_ref)[row // 3]
        picked = [source[row % 3, 0, 0, k].astype(F32) for k in range(4)]
        value = jnp.where(
            sphere < 2,
            jnp.where(sphere == 0, picked[0], picked[1]),
            jnp.where(sphere == 2, picked[2], picked[3]),
        )
        state[row : row + 1, :] = value
    pl.semaphore_wait(barrier, 8)

    state_copies = {}
    for n, d in enumerate(DIRECTIONS):
        there = 8 - d
        state_copies[there] = pltpu.make_async_remote_copy(
            src_ref=state, dst_ref=states.at[there],
            send_sem=state_send.at[n], recv_sem=state_recv.at[there],
            device_id=neighbour(d), device_id_type=MESH,
        )
        state_copies[there].start()

    which = lax.broadcasted_iota(jnp.int32, (16, LANES), 0)
    rates = jnp.zeros((16, LANES), F32)
    for r in range(15):
        rates = jnp.where(which == r, rates_ref[r], rates)
    coef[...] = jnp.dot(
        coef_in[...], rates, precision=lax.Precision.HIGHEST, preferred_element_type=F32
    )

    get_codes.wait()
    slot_rows = lax.broadcasted_iota(jnp.int32, (48, CELLS), 0)

    def fill_onehot(step, carry):
        layer, row = step // CX, lax.rem(step, CX)
        slots = codes[layer, pl.ds(row, 1), :] >> 8
        hit = jnp.where(slots == slot_rows, 1.0, 0.0)
        onehot[:, pl.ds(pl.multiple_of(step * CELLS, CELLS), CELLS)] = hit.astype(jnp.bfloat16)
        return carry

    lax.fori_loop(0, 2 * CX, fill_onehot, 0)

    get_pops.wait()

    def fluid(chunk, carry):
        at = pl.ds(pl.multiple_of(chunk * LANES, LANES), LANES)
        p = [f[i, :, at] for i in range(19)]
        s = {a: p[a] + p[a + 1] for a in range(1, 19, 2)}
        d = {a: p[a] - p[a + 1] for a in range(1, 19, 2)}
        s_xy, a_xy = s[7] + s[9], s[7] - s[9]
        s_xz, a_xz = s[11] + s[13], s[11] - s[13]
        s_yz, a_yz = s[15] + s[17], s[15] - s[17]
        x1, x2 = d[7] + d[9], d[11] + d[13]
        y1, y2 = d[7] - d[9], d[15] + d[17]
        z1, z2 = d[11] - d[13], d[15] - d[17]
        density = (p[0] + s[1]) + (s[3] + s[5]) + (s_xy + s_xz) + s_yz
        jx, jy, jz = d[1] + x1 + x2, d[3] + y1 + y2, d[5] + z1 + z2
        inverse = 1.0 / density
        ux, uy, uz = jx * inverse, jy * inverse, jz * inverse
        for n, value in enumerate((density, jx, jy, jz, ux, uy, uz)):
            moments[n, :, at] = value
        cover = ((codes[0, :, at] & 255) + (codes[1, :, at] & 255)).astype(F32) * (1.0 / 255.0)
        keep = 1.0 - cover
        hx, hy, hz = 0.5 * jx * ux, 0.5 * jy * uy, 0.5 * jz * uz
        base = density * (1.0 / 9.0) - (hx + hy + hz) * (1.0 / 3.0)
        even = [
            s[1] - base - hx,
            s[3] - base - hy,
            s[5] - base - hz,
            s_xy - base - (hx + hy),
            s_xz - base - (hx + hz),
            s_yz - base - (hy + hz),
        ]
        even = [keep * value for value in even]

        def c(n):
            return jnp.broadcast_to(coef[n : n + 1, :], (CX, LANES))

        sums = []
        for a in range(6):
            total = c(6 * a) * even[0]
            for b in range(1, 6):
                total = total + c(6 * a + b) * even[b]
            sums.append(total)
        third = 1.0 / 3.0
        odd = []
        for axis, (first, second, flow) in enumerate(((x1, x2, jx), (y1, y2, jy), (z1, z2, jz))):
            level = flow * third
            first, second = keep * (first - level), keep * (second - level)
            k = 36 + 4 * axis
            near = c(k) * first + c(k + 1) * second
            far = c(k + 2) * first + c(k + 3) * second
            odd.append((-2.0 * (near + far), near, far))
        n_xy = keep * (a_xy - jx * uy) * c(48)
        n_xz = keep * (a_xz - jx * uz) * c(49)
        n_yz = keep * (a_yz - jy * uz) * c(50)
        post[0, :, at] = p[0] + 2.0 * (sums[0] + sums[1] + sums[2]) + 4.0 * (sums[3] + sums[4] + sums[5])
        pairs = {
            1: (sums[0], odd[0][0]),
            3: (sums[1], odd[1][0]),
            5: (sums[2], odd[2][0]),
            7: (sums[3] + n_xy, odd[0][1] + odd[1][1]),
            9: (sums[3] - n_xy, odd[0][1] - odd[1][1]),
            11: (sums[4] + n_xz, odd[0][2] + odd[2][1]),
            13: (sums[4] - n_xz, odd[0][2] - odd[2][1]),
            15: (sums[5] + n_yz, odd[1][2] + odd[2][2]),
            17: (sums[5] - n_yz, odd[1][2] - odd[2][2]),
        }
        for a, (ev, od) in pairs.items():
            od = od + cover * d[a]
            post[a, :, at] = p[a] - ev - od
            post[a + 1, :, at] = p[a + 1] - ev + od
        return carry

    lax.fori_loop(0, CHUNKS, fluid, 0)
    contrib[:, 48:64, :] = jnp.zeros((2 * CHUNKS, 16, LANES), F32)

    for there in DIRECTIONS:
        state_copies[there].wait()
    lanes16 = lax.broadcasted_iota(jnp.int32, (16, LANES), 1)
    group = lanes16 >> 2
    rows16 = lax.broadcasted_iota(jnp.int32, (16, LANES), 0)
    full = jnp.where(group == 4, state[...], 0.0)
    for d in DIRECTIONS:
        full = jnp.where(group == d, states[d], full)
    off_x = jnp.where(group >= 6, CX, jnp.where(group >= 3, 0, -CX)).astype(F32)
    third_of = group - jnp.where(group >= 6, 6, jnp.where(group >= 3, 3, 0))
    off_y = ((third_of - 1) * CY).astype(F32)
    full = full + jnp.where(rows16 == 0, off_x, jnp.where(rows16 == 1, off_y, 0.0))
    table[...] = full

    def covers(chunk, carry):
        start = pl.multiple_of(chunk * LANES, LANES)
        at = pl.ds(start, LANES)
        lanes = lax.broadcasted_iota(jnp.int32, (CX, LANES), 1)
        cell_x = lax.broadcasted_iota(jnp.int32, (CX, LANES), 0).astype(F32)
        cell_y = ((lanes >> 6) + 2 * chunk).astype(F32)
        cell_z = (lanes & 63).astype(F32)
        density, jx, jy, jz, ux, uy, uz = [moments[n, :, at] for n in range(7)]
        first = second = None
        for layer in range(2):
            packed = codes[layer, :, at]
            slot = packed >> 8
            eps = (packed & 255).astype(F32) * (1.0 / 255.0)
            got = [
                jnp.take_along_axis(
                    jnp.broadcast_to(table[n : n + 1, :], (CX, LANES)), slot,
                    axis=1, mode="promise_in_bounds",
                )
                for n in range(9)
            ]
            rx, ry, rz = cell_x - got[0], cell_y - got[1], cell_z - got[2]
            wx = got[3] + got[7] * rz - got[8] * ry
            wy = got[4] + got[8] * rx - got[6] * rz
            wz = got[5] + got[6] * ry - got[7] * rx
            weight = eps * density
            bx, by, bz = weight * wx, weight * wy, weight * wz
            fx, fy, fz = eps * jx - bx, eps * jy - by, eps * jz - bz
            rows = (fx, fy, fz, ry * fz - rz * fy, rz * fx - rx * fz, rx * fy - ry * fx)
            for n, value in enumerate(rows):
                contrib[layer * CHUNKS + chunk, CX * n : CX * (n + 1), :] = value
            quad = (bx * wx, by * wy, bz * wz, bx * wy, bx * wz, by * wz)
            if layer == 0:
                first, second, cover = (bx, by, bz), quad, eps
            else:
                first = [a + b for a, b in zip(first, (bx, by, bz))]
                second = [a + b for a, b in zip(second, quad)]
                cover = cover + eps
        ex, ey, ez = cover * jx, cover * jy, cover * jz
        hx, hy, hz = first[0] + ex, first[1] + ey, first[2] + ez
        qxx, qyy, qzz = second[0] - ex * ux, second[1] - ey * uy, second[2] - ez * uz
        qxy, qxz, qyz = second[3] - ex * uy, second[4] - ex * uz, second[5] - ey * uz
        trace = qxx + qyy + qzz
        post[0, :, at] = post[0, :, at] - 0.5 * trace
        axis_base = trace * (-1.0 / 12.0)
        half_base = trace * (-1.0 / 24.0)
        hx, hy, hz = hx * (1.0 / 12.0), hy * (1.0 / 12.0), hz * (1.0 / 12.0)
        exx, eyy, ezz = 0.125 * qxx, 0.125 * qyy, 0.125 * qzz
        exy, exz, eyz = 0.25 * qxy, 0.25 * qxz, 0.25 * qyz
        b_xy, b_xz, b_yz = half_base + exx + eyy, half_base + exx + ezz, half_base + eyy + ezz
        pairs = {
            1: (axis_base + 2.0 * exx, 2.0 * hx),
            3: (axis_base + 2.0 * eyy, 2.0 * hy),
            5: (axis_base + 2.0 * ezz, 2.0 * hz),
            7: (b_xy + exy, hx + hy),
            9: (b_xy - exy, hx - hy),
            11: (b_xz + exz, hx + hz),
            13: (b_xz - exz, hx - hz),
            15: (b_yz + eyz, hy + hz),
            17: (b_yz - eyz, hy - hz),
        }
        for a, (ev, od) in pairs.items():
            post[a, :, at] = post[a, :, at] + (ev + od)
            post[a + 1, :, at] = post[a + 1, :, at] + (ev - od)
        return carry

    lax.fori_loop(0, CHUNKS, covers, 0)

    def passed(pop):
        value = post[pop]
        shift = lane_shift(pop) % CELLS
        if shift:
            value = pltpu.roll(value, shift, 1)
        step = int(VELOCITIES[pop, 0]) % CX
        if step:
            value = pltpu.roll(value, step, 0)
        return value

    z_of = lax.broadcasted_iota(jnp.int32, (CX, CELLS), 1) & (NZ - 1)
    edge = {1: z_of == 0, -1: z_of == NZ - 1}
    lower = lax.broadcasted_iota(jnp.int32, (1, LANES), 1) < NZ
    corners = {}
    for pop in range(19):
        step_x, step_y, step_z = (int(v) for v in VELOCITIES[pop])
        value = passed(pop)
        if step_x:
            row = 0 if step_x > 0 else CX - 1
            side = 0 if step_x > 0 else 1
            n = (X_UP, X_DOWN)[side].index(pop)
            for c in range(CHUNKS):
                xsend[side, n * CHUNKS + c : n * CHUNKS + c + 1, :] = value[
                    row : row + 1, c * LANES : (c + 1) * LANES
                ]
        if step_y:
            side = 0 if step_y > 0 else 1
            n = (Y_UP, Y_DOWN)[side].index(pop)
            c = 0 if step_y > 0 else CHUNKS - 1
            ysend[side, n] = value[:, c * LANES : (c + 1) * LANES]
            if step_x:
                corners[pop] = value[row : row + 1, c * LANES : (c + 1) * LANES]
        if step_z:
            value = jnp.where(edge[step_z], post[OPPOSITE[pop]], value)
        out[pop] = value
    loads[6:7, :] = jnp.where(lower, corners[7], corners[8])
    loads[7:8, :] = jnp.where(lower, corners[10], corners[9])

    halo = []
    for n, (src, dst, d) in enumerate(
        (
            (xsend.at[0], xrecv.at[0], 7),
            (xsend.at[1], xrecv.at[1], 1),
            (ysend.at[0], yrecv.at[0], 5),
            (ysend.at[1], yrecv.at[1], 3),
        )
    ):
        halo.append(
            pltpu.make_async_remote_copy(
                src_ref=src, dst_ref=dst, send_sem=halo_send.at[n], recv_sem=halo_recv.at[n],
                device_id=neighbour(d), device_id_type=MESH,
            )
        )
        halo[-1].start()

    for layer in range(2):
        for row in range(CX):
            for c in range(CHUNKS):
                value = contrib[layer * CHUNKS + c, pl.ds(row, 8, stride=CX), :]
                high = value.astype(jnp.bfloat16).astype(F32)
                both = jnp.concatenate([high, value - high], axis=0)
                at = (layer * CX + row) * CELLS + c * LANES
                split[:, at : at + LANES] = both.astype(jnp.bfloat16)
    sums = lax.dot_general(
        split[...], onehot[...], (((1,), (1,)), ((), ())), preferred_element_type=F32
    )
    sums = sums[0:8] + sums[8:16]
    row8 = lax.broadcasted_iota(jnp.int32, (8, 48), 0)
    sums = sums * jnp.where(row8 < 3, 1.0 / RADIUS**2, 1.0 / RADIUS**3)
    loads[0:6, 0:48] = sums[0:6]

    load_copies = {}
    for n, d in enumerate(DIRECTIONS):
        there = 8 - d
        load_copies[there] = pltpu.make_async_remote_copy(
            src_ref=loads, dst_ref=loads_in.at[there],
            send_sem=load_send.at[n], recv_sem=load_recv.at[there],
            device_id=neighbour(d), device_id_type=MESH,
        )
        load_copies[there].start()

    for copy in halo:
        copy.wait()
    for side, names in enumerate((X_UP, X_DOWN)):
        row = 0 if side == 0 else CX - 1
        for n, pop in enumerate(names):
            step_z = int(VELOCITIES[pop, 2])
            for c in range(CHUNKS):
                at = slice(c * LANES, (c + 1) * LANES)
                value = xrecv[side, n * CHUNKS + c : n * CHUNKS + c + 1, :]
                if step_z:
                    value = jnp.where(edge[step_z][0:1, at], out[pop, row : row + 1, at], value)
                out[pop, row : row + 1, at] = value
    lower8 = lax.broadcasted_iota(jnp.int32, (CX, LANES), 1) < NZ
    for side, names in enumerate((Y_UP, Y_DOWN)):
        c = 0 if side == 0 else CHUNKS - 1
        at = slice(c * LANES, (c + 1) * LANES)
        for n, pop in enumerate(names):
            step_z = int(VELOCITIES[pop, 2])
            mask = lower8 if side == 0 else jnp.logical_not(lower8)
            if step_z:
                mask = jnp.logical_and(mask, jnp.logical_not(edge[step_z][:, at]))
            out[pop, :, at] = jnp.where(mask, yrecv[side, n], out[pop, :, at])

    for there in DIRECTIONS:
        load_copies[there].wait()
    for pop, source, row, c, corner_row in (
        (7, 0, 0, 0, 6),
        (8, 8, CX - 1, CHUNKS - 1, 6),
        (9, 2, 0, CHUNKS - 1, 7),
        (10, 6, CX - 1, 0, 7),
    ):
        at = slice(c * LANES, (c + 1) * LANES)
        mask = lower if c == 0 else jnp.logical_not(lower)
        out[pop, row : row + 1, at] = jnp.where(
            mask, loads_in[source, corner_row : corner_row + 1, :], out[pop, row : row + 1, at]
        )
    put = pltpu.make_async_copy(out, out_hbm, out_sem.at[0])
    put.start()

    total = None
    for d in range(9):
        tile = loads[...] if d == 4 else loads_in[d]
        back = (4 * (8 - d)) % LANES
        tile = pltpu.roll(tile, (LANES - back) % LANES, 1) if back else tile
        total = tile if total is None else total + tile
    for row in range(6):
        load_ref[row, 0, :, :] = total[row : row + 1, 0:4]
    put.wait()


def per_device(populations, cover_codes, sphere_cell, sphere_velocity, sphere_spin, relax_rates):
    vmem, smem, anywhere = (
        pl.BlockSpec(memory_space=pltpu.VMEM),
        pl.BlockSpec(memory_space=pltpu.SMEM),
        pl.BlockSpec(memory_space=pl.ANY),
    )
    dma = pltpu.SemaphoreType.DMA
    return pl.pallas_call(
        kernel,
        out_shape=(
            jax.ShapeDtypeStruct((19, CX, CELLS), F32),
            jax.ShapeDtypeStruct((6, 1, 1, 4), F32),
        ),
        in_specs=[anywhere, anywhere, smem, smem, smem, smem, vmem],
        out_specs=(anywhere, vmem),
        scratch_shapes=[
            pltpu.VMEM((19, CX, CELLS), F32),
            pltpu.VMEM((2, CX, CELLS), jnp.int32),
            pltpu.VMEM((64, LANES), F32),
            pltpu.VMEM((19, CX, CELLS), F32),
            pltpu.VMEM((7, CX, CELLS), F32),
            pltpu.VMEM((48, 2 * CX * CELLS), jnp.bfloat16),
            pltpu.VMEM((2 * CHUNKS, 64, LANES), F32),
            pltpu.VMEM((16, 2 * CX * CELLS), jnp.bfloat16),
            pltpu.VMEM((19, CX, CELLS), F32),
            pltpu.VMEM((16, LANES), F32),
            pltpu.VMEM((9, 16, LANES), F32),
            pltpu.VMEM((16, LANES), F32),
            pltpu.VMEM((2, 40, LANES), F32),
            pltpu.VMEM((2, 40, LANES), F32),
            pltpu.VMEM((2, 5, CX, LANES), F32),
            pltpu.VMEM((2, 5, CX, LANES), F32),
            pltpu.VMEM((8, LANES), F32),
            pltpu.VMEM((9, 8, LANES), F32),
            dma((2,)),
            dma((1,)),
            dma((8,)),
            dma((9,)),
            dma((4,)),
            dma((4,)),
            dma((8,)),
            dma((9,)),
        ],
        compiler_params=pltpu.CompilerParams(
            collective_id=0, has_side_effects=True, vmem_limit_bytes=32 * 1024 * 1024
        ),
    )(
        populations, cover_codes, sphere_cell, sphere_velocity, sphere_spin, relax_rates,
        jnp.asarray(coefficient_rows()),
    )


def solution(mesh):
    placed = (
        P(None, "bx", "by"),
        P(None, "bx", "by"),
        P(None, "bx", "by", None),
        P(None, "bx", "by", None),
        P(None, "bx", "by", None),
        P(),
    )
    return jax.shard_map(
        per_device,
        mesh=mesh,
        in_specs=placed,
        out_specs=(P(None, "bx", "by"), P(None, "bx", "by", None)),
        check_vma=False,
    )
```

time: 86.3 us -> 42.4 us (0.49)
  starting transfers between devices: 48.8 us -> 0 us
  Pallas kernels: 0 us -> 34.6 us
  local copies, waits for them, and re-layouts: 21.4 us -> 6.85 us
  other arithmetic: 7.67 us -> 0 us
  matrix products: 3.96 us -> 0 us
  waiting for transfers between devices: 2.31 us -> 0 us
  between operations: 1.57 us -> 0.65 us
    ppermute x12 -> x0, starting transfers between devices: 48.8 us -> none  [the longest x6 38.4 us: padded(): after = lax.ppermute(first, axis, down)]
    pallas_call x0 -> x1, Pallas kernels: none -> 34.6 us  [per_device(): pl.pallas_call(kernel, out_shape=(jax.ShapeDtypeStruct((19, CX, CELLS), F...]
    unnamed x31 -> x15, local copies, waits for them, and re-layouts: 13.3 us -> 6.19 us
    dot_general x6 -> x0, matrix products: 3.96 us -> none  [the longest x2 1.56 us: collide_block(): jnp.einsum('sxc,kxc->sk', onehot, contrib, precision=lax.Precision.HIGHEST)]
    unnamed x74 -> x0, other arithmetic: 2.96 us -> none
    slice x22 -> x0, local copies, waits for them, and re-layouts: 2.75 us -> none  [the longest x10 0.78 us: along_z(): return jnp.concatenate([shifted[..., 1:], bounce[..., -1:]], axis=-1)]
    ppermute x12 -> x0, waiting for transfers between devices: 2.31 us -> none  [the longest x6 1.92 us: padded(): before = lax.ppermute(last, axis, up)]
    another operation x20 -> x0, local copies, waits for them, and re-layouts: 2.16 us -> none  [the longest x19 2.12 us: per_device(): populations_next = jnp.stack(passed).reshape(pop_total, width_x, flat_cells)]
  transfers between devices with their start and end apart: 12 -> 0, of which waited for: 5 -> 0; matrix products, arithmetic and copies ran while one was open for 12% -> 0% of each run, Pallas kernels for 0% -> 0%
where the time goes in v1:
time: 42.4 us; the launch traced here: 42.1 us
  Pallas kernels  34.6 us (82%)
  local copies, waits for them, and re-layouts  6.85 us (16%)
  between operations  0.65 us (2%)
    pallas_call x1, Pallas kernels, per_device(): pl.pallas_call(kernel, out_shape=(jax.ShapeDtypeStruct((19, CX, CELLS), F...  34.6 us
    unnamed x15, local copies, waits for them, and re-layouts  6.19 us

profile of v1, /device:TPU:1, one launch (start us, length us, event | category | flops | bytes accessed | tf_op | source)
XLA Modules:
  0.0 42.1 jit_solution(10410397620287079909)
XLA Ops:
  0.6 0.0 copy-start
  0.6 1.1 %copy-done = f32[19,8,1024]{2,1,0:T(8,128)S(1)} copy-done((f32[19,8,1024]{2,1,0:T(8,128)S(1)}, f32[19,8,1024]{2,1,0:T(8,128)}, u32[]{:S(2)}) %copy-start) | copy-done | bytes 622616
  1.7 0.0 copy-start.1
  1.7 0.8 %copy-done.1 = s32[2,8,1024]{2,1,0:T(8,128)S(1)} copy-done((s32[2,8,1024]{2,1,0:T(8,128)S(1)}, s32[2,8,1024]{2,1,0:T(8,128)}, u32[]{:S(2)}) %copy-start.1) | copy-done | bytes 65560
  2.5 0.0 copy-start.2
  2.6 0.8 %copy-done.2 = f32[64,16]{1,0:T(8,128)S(1)} copy-done((f32[64,16]{1,0:T(8,128)S(1)}, f32[64,16]{1,0:T(8,128)}, u32[]{:S(2)}) %copy-start.2) | copy-done | bytes 4120
  3.3 0.0 copy-start.3
  3.3 0.7 %copy-done.3 = s32[3,1,1,4]{3,2,1,0:T(1,128)S(1)} copy-done((s32[3,1,1,4]{3,2,1,0:T(1,128)S(1)}, s32[3,1,1,4]{3,2,1,0:T(1,128)}, u32[]{:S(2)}) %copy-start.3) | copy-done | bytes 72
  4.0 0.0 copy-start.4
  4.0 0.7 %copy-done.4 = f32[3,1,1,4]{3,2,1,0:T(1,128)S(1)} copy-done((f32[3,1,1,4]{3,2,1,0:T(1,128)S(1)}, f32[3,1,1,4]{3,2,1,0:T(1,128)}, u32[]{:S(2)}) %copy-start.4) | copy-done | bytes 72
  4.7 0.0 copy-start.5
  4.7 0.7 %copy-done.5 = f32[3,1,1,4]{3,2,1,0:T(1,128)S(1)} copy-done((f32[3,1,1,4]{3,2,1,0:T(1,128)S(1)}, f32[3,1,1,4]{3,2,1,0:T(1,128)}, u32[]{:S(2)}) %copy-start.5) | copy-done | bytes 72
  5.3 0.0 copy-start.6
  5.4 0.7 %copy-done.6 = f32[15]{0:T(128)S(1)} copy-done((f32[15]{0:T(128)S(1)}, f32[15]{0:T(128)}, u32[]{:S(2)}) %copy-start.6) | copy-done | bytes 84
  6.0 34.6 %shard_map.86 = (f32[19,8,1024]{2,1,0:T(8,128)S(1)}, f32[6,1,1,4]{3,2,1,0:T(1,128)S(1)}) custom-call(f32[19,8,1024]{2,1,0:T(8,128)S(1)} %copy-done, s32[2,8,1024]{2,1,0:T(8,128)S(1)} %copy-done.1, s32[3,1,1,4]{3,2,1,0:T(1,128)S(1)} %copy-done.3, f32[3,1,1,4]{3,2,1,0:T(1,128)S(1)} %copy-done.4, f32[3,1,1,4]{3,2,1,0:T(1,128)S(1)} %copy-done.5, ...), custom_call_target="tpu_custom_call" | custom-call | tf_op jit(solution)/shard_map/pallas_call | solution.py:461
  40.6 0.7 %copy.9 = f32[6,1,1,4]{0,3,2,1:T(4,128)} copy(f32[6,1,1,4]{3,2,1,0:T(1,128)S(1)} %get-tuple-element.3) | data formatting | bytes 192 | tf_op jit(solution)/shard_map/pallas_call | solution.py:461
  41.2 0.8 %copy.11 = f32[19,8,1024]{2,1,0:T(8,128)} copy(f32[19,8,1024]{2,1,0:T(8,128)S(1)} %get-tuple-element.6) | data formatting | bytes 1245184
Async XLA Ops:
  0.6 1.1 %copy-start = (f32[19,8,1024]{2,1,0:T(8,128)S(1)}, f32[19,8,1024]{2,1,0:T(8,128)}, u32[]{:S(2)}) copy-start(f32[19,8,1024]{2,1,0:T(8,128)} %pops_hbm.1) | copy-start | bytes 1867780
  1.7 0.8 %copy-start.1 = (s32[2,8,1024]{2,1,0:T(8,128)S(1)}, s32[2,8,1024]{2,1,0:T(8,128)}, u32[]{:S(2)}) copy-start(s32[2,8,1024]{2,1,0:T(8,128)} %codes_hbm.1) | copy-start | bytes 196612
  2.5 0.8 %copy-start.2 = (f32[64,16]{1,0:T(8,128)S(1)}, f32[64,16]{1,0:T(8,128)}, u32[]{:S(2)}) copy-start(f32[64,16]{1,0:T(8,128)} %constant.2.clone.coef_in) | copy-start | bytes 12292
  3.3 0.7 %copy-start.3 = (s32[3,1,1,4]{3,2,1,0:T(1,128)S(1)}, s32[3,1,1,4]{3,2,1,0:T(1,128)}, u32[]{:S(2)}) copy-start(s32[3,1,1,4]{3,2,1,0:T(1,128)} %cell_ref.1) | copy-start | bytes 148
  4.0 0.7 %copy-start.4 = (f32[3,1,1,4]{3,2,1,0:T(1,128)S(1)}, f32[3,1,1,4]{3,2,1,0:T(1,128)}, u32[]{:S(2)}) copy-start(f32[3,1,1,4]{3,2,1,0:T(1,128)} %vel_ref.1) | copy-start | bytes 148
  4.7 0.7 %copy-start.5 = (f32[3,1,1,4]{3,2,1,0:T(1,128)S(1)}, f32[3,1,1,4]{3,2,1,0:T(1,128)}, u32[]{:S(2)}) copy-start(f32[3,1,1,4]{3,2,1,0:T(1,128)} %spin_ref.1) | copy-start | bytes 148
  5.3 0.7 %copy-start.6 = (f32[15]{0:T(128)S(1)}, f32[15]{0:T(128)}, u32[]{:S(2)}) copy-start(f32[15]{0:T(128)} %rates_ref.1) | copy-start | bytes 184

commit v2 on v1

--- a/solution.py
+++ b/solution.py
@@ -102,8 +102,8 @@
 
 def kernel(
     pops_hbm, codes_hbm, cell_ref, vel_ref, spin_ref, rates_ref, coef_in,
-    out_hbm, load_ref,
-    f, codes, coef, post, moments, onehot, contrib, split, out,
+    out, load_ref,
+    f, codes, coef, post, moments, onehot, contrib, split,
     state, states, table, xsend, xrecv, ysend, yrecv, loads, loads_in,
     in_sem, out_sem, state_send, state_recv, halo_send, halo_recv, load_send, load_recv,
 ):
@@ -437,8 +437,6 @@
         out[pop, row : row + 1, at] = jnp.where(
             mask, loads_in[source, corner_row : corner_row + 1, :], out[pop, row : row + 1, at]
         )
-    put = pltpu.make_async_copy(out, out_hbm, out_sem.at[0])
-    put.start()
 
     total = None
     for d in range(9):
@@ -446,9 +444,7 @@
         back = (4 * (8 - d)) % LANES
         tile = pltpu.roll(tile, (LANES - back) % LANES, 1) if back else tile
         total = tile if total is None else total + tile
-    for row in range(6):
-        load_ref[row, 0, :, :] = total[row : row + 1, 0:4]
-    put.wait()
+    load_ref[...] = total.T[0:4, 0:6]
 
 
 def per_device(populations, cover_codes, sphere_cell, sphere_velocity, sphere_spin, relax_rates):
@@ -458,14 +454,14 @@
         pl.BlockSpec(memory_space=pl.ANY),
     )
     dma = pltpu.SemaphoreType.DMA
-    return pl.pallas_call(
+    out, load = pl.pallas_call(
         kernel,
         out_shape=(
-            jax.ShapeDtypeStruct((19, CX, CELLS), F32),
-            jax.ShapeDtypeStruct((6, 1, 1, 4), F32),
+            pltpu.VMEM((19, CX, CELLS), F32),
+            jax.ShapeDtypeStruct((4, 6), F32),
         ),
         in_specs=[anywhere, anywhere, smem, smem, smem, smem, vmem],
-        out_specs=(anywhere, vmem),
+        out_specs=(vmem, vmem),
         scratch_shapes=[
             pltpu.VMEM((19, CX, CELLS), F32),
             pltpu.VMEM((2, CX, CELLS), jnp.int32),
@@ -475,7 +471,6 @@
             pltpu.VMEM((48, 2 * CX * CELLS), jnp.bfloat16),
             pltpu.VMEM((2 * CHUNKS, 64, LANES), F32),
             pltpu.VMEM((16, 2 * CX * CELLS), jnp.bfloat16),
-            pltpu.VMEM((19, CX, CELLS), F32),
             pltpu.VMEM((16, LANES), F32),
             pltpu.VMEM((9, 16, LANES), F32),
             pltpu.VMEM((16, LANES), F32),
@@ -495,12 +490,13 @@
             dma((9,)),
         ],
         compiler_params=pltpu.CompilerParams(
-            collective_id=0, has_side_effects=True, vmem_limit_bytes=32 * 1024 * 1024
+            collective_id=0, has_side_effects=True, vmem_limit_bytes=60 * 1024 * 1024
         ),
     )(
         populations, cover_codes, sphere_cell, sphere_velocity, sphere_spin, relax_rates,
         jnp.asarray(coefficient_rows()),
     )
+    return out, load.T.reshape(6, 1, 1, 4)
 
 
 def solution(mesh):

time: 42.4 us -> 37.4 us (0.88)
  local copies, waits for them, and re-layouts: 6.85 us -> 1.41 us
  Pallas kernels: 34.6 us -> 35.1 us
    unnamed x15 -> x4, local copies, waits for them, and re-layouts: 6.19 us -> 1.41 us
    pallas_call x1 -> x0, local copies, waits for them, and re-layouts: 0.66 us -> none  [per_device(): pl.pallas_call(kernel, out_shape=(jax.ShapeDtypeStruct((19, CX, CELLS), F...]
    pallas_call x1, Pallas kernels: 34.6 us -> 35.1 us  [per_device(): pl.pallas_call(kernel, out_shape=(pltpu.VMEM((19, CX, CELLS), F32), jax.S...]
where the time goes in v2:
time: 37.4 us; the launch traced here: 37.2 us
  Pallas kernels  35.1 us (94%)
  local copies, waits for them, and re-layouts  1.41 us (4%)
  between operations  0.65 us (2%)
    pallas_call x1, Pallas kernels, per_device(): pl.pallas_call(kernel, out_shape=(pltpu.VMEM((19, CX, CELLS), F32), jax.S...  35.1 us
    unnamed x4, local copies, waits for them, and re-layouts  1.41 us

profile of v2, /device:TPU:1, one launch (start us, length us, event | category | flops | bytes accessed | tf_op | source)
XLA Modules:
  0.0 37.2 jit_solution(16442913425700680607)
XLA Ops:
  0.6 35.1 %shard_map.86 = (f32[19,8,1024]{2,1,0:T(8,128)S(1)}, f32[4,6]{1,0:T(4,128)}) custom-call(f32[19,8,1024]{2,1,0:T(8,128)} %pops_hbm.1, s32[2,8,1024]{2,1,0:T(8,128)} %codes_hbm.1, s32[3,1,1,4]{3,2,1,0:T(1,128)} %cell_ref.1, f32[3,1,1,4]{3,2,1,0:T(1,128)} %vel_ref.1, f32[3,1,1,4]{3,2,1,0:T(1,128)} %spin_ref.1, f32[15]{0:T(128)} %rates_ref.1, ...), custom_call_target="tpu_custom_call" | custom-call | tf_op jit(solution)/shard_map/pallas_call | solution.py:457
  35.8 0.0 copy-start
  35.8 0.8 %copy.11 = f32[19,8,1024]{2,1,0:T(8,128)} copy(f32[19,8,1024]{2,1,0:T(8,128)S(1)} %get-tuple-element.6) | data formatting | bytes 1245184
  36.6 0.0 copy-done
  36.6 0.6 %copy.12 = f32[6,1,1,4]{0,3,2,1:T(4,128)} copy(f32[6,1,1,4]{0,3,2,1:T(4,128)S(1)} %bitcast.3) | data formatting | bytes 192
Async XLA Ops:
  35.8 0.8 %copy-start = (f32[4,6]{1,0:T(4,128)S(1)}, f32[4,6]{1,0:T(4,128)}, u32[]{:S(2)}) copy-start(f32[4,6]{1,0:T(4,128)} %get-tuple-element.5) | copy-start | bytes 292

commit v3 on v2

v3 whole, which is shorter than its diff:
```python
import jax
import jax.numpy as jnp
import numpy as np
from jax import lax
from jax.experimental import pallas as pl
from jax.experimental.pallas import tpu as pltpu
from jax.sharding import PartitionSpec as P

NZ = 64
RADIUS = 8
CX, CY = 8, 16
CELLS = CY * NZ
LANES = 128
CHUNKS = CELLS // LANES
MESH = pl.DeviceIdType.MESH
F32 = jnp.float32

VELOCITIES = np.array(
    [
        [0, 0, 0],
        [1, 0, 0],
        [-1, 0, 0],
        [0, 1, 0],
        [0, -1, 0],
        [0, 0, 1],
        [0, 0, -1],
        [1, 1, 0],
        [-1, -1, 0],
        [1, -1, 0],
        [-1, 1, 0],
        [1, 0, 1],
        [-1, 0, -1],
        [1, 0, -1],
        [-1, 0, 1],
        [0, 1, 1],
        [0, -1, -1],
        [0, 1, -1],
        [0, -1, 1],
    ]
)
OPPOSITE = [0, 2, 1, 4, 3, 6, 5, 8, 7, 10, 9, 12, 11, 14, 13, 16, 15, 18, 17]
X_UP, X_DOWN = (1, 7, 9, 11, 13), (2, 8, 10, 12, 14)
Y_UP, Y_DOWN = (3, 7, 10, 15, 17), (4, 8, 9, 16, 18)
NEAR = [(dx, dy) for dx in range(-2, 3) for dy in range(-1, 2)]
HERE = NEAR.index((0, 0))
SENDS = [0, 2, 12, 14, 3, 5, 9, 11, 1, 13, 4, 10, 6, 8]
BESIDE = [t for t in SENDS if abs(NEAR[t][0]) < 2]
CORNERS = {7: (-1, -1), 8: (1, 1), 9: (-1, 1), 10: (1, -1)}
MOMENTS = 16
ROWS = 48


def moment_rows():
    vel_x, vel_y, vel_z = [VELOCITIES[:, component] * 1.0 for component in range(3)]
    monomials = [
        np.ones(19),
        vel_x,
        vel_y,
        vel_z,
        vel_x * vel_x,
        vel_y * vel_y,
        vel_z * vel_z,
        vel_x * vel_y,
        vel_x * vel_z,
        vel_y * vel_z,
        vel_x * vel_x * vel_y,
        vel_x * vel_x * vel_z,
        vel_y * vel_y * vel_x,
        vel_y * vel_y * vel_z,
        vel_z * vel_z * vel_x,
        vel_z * vel_z * vel_y,
        vel_x * vel_x * vel_y * vel_y,
        vel_x * vel_x * vel_z * vel_z,
        vel_y * vel_y * vel_z * vel_z,
    ]
    orthonormal = []
    for vector in monomials:
        vector = vector.copy()
        for earlier in orthonormal:
            vector = vector - np.dot(earlier, vector) * earlier
        orthonormal.append(vector / np.sqrt(np.dot(vector, vector)))
    return np.stack(orthonormal)


def coefficient_rows():
    rows = moment_rows()[4:]
    even = [1, 3, 5, 7, 11, 15]
    out = []
    for a in even:
        for b in even:
            keep = np.isin(np.arange(15), [0, 1, 2, 12, 13, 14])
            out.append(rows[:, a] * (rows[:, b] - rows[:, 0]) * keep)
    for axis, first, second, rates in ((1, 7, 11, (8, 10)), (3, 7, 15, (6, 11)), (5, 11, 15, (7, 9))):
        for a in (first, second):
            for b in (first, second):
                keep = np.isin(np.arange(15), rates)
                out.append(rows[:, a] * (rows[:, b] - rows[:, axis]) * keep)
    for rate in (3, 4, 5):
        out.append(0.25 * (np.arange(15) == rate))
    table = np.zeros((64, 16), np.float32)
    table[: len(out), :15] = np.stack(out)
    return table


def lane_shift(pop):
    return int(VELOCITIES[pop, 1]) * NZ + int(VELOCITIES[pop, 2])


def sphere_terms(density, codes, table, cell, first_slot):
    flow, square, cover = None, None, None
    for packed in codes:
        slot = (packed >> 8) + first_slot
        weight = (packed & 255).astype(F32) * (1.0 / 255.0) * density
        got = [
            jnp.take_along_axis(
                jnp.broadcast_to(table[n : n + 1, :], (CX, LANES)), slot,
                axis=1, mode="promise_in_bounds",
            )
            for n in range(9)
        ]
        rx, ry, rz = cell[0] - got[0], cell[1] - got[1], cell[2] - got[2]
        wx = got[3] + got[7] * rz - got[8] * ry
        wy = got[4] + got[8] * rx - got[6] * rz
        wz = got[5] + got[6] * ry - got[7] * rx
        bx, by, bz = weight * wx, weight * wy, weight * wz
        one = (bx, by, bz)
        two = (bx * wx, by * wy, bz * wz, bx * wy, bx * wz, by * wz)
        if flow is None:
            flow, square, cover = one, two, weight
        else:
            flow = [a + b for a, b in zip(flow, one)]
            square = [a + b for a, b in zip(square, two)]
            cover = cover + weight
    hx, hy, hz = [value * (1.0 / 12.0) for value in flow]
    qxx, qyy, qzz, qxy, qxz, qyz = square
    base = cover * (1.0 / 18.0) - (qxx + qyy + qzz) * (1.0 / 12.0)
    half = 0.5 * base
    exx, eyy, ezz = 0.125 * qxx, 0.125 * qyy, 0.125 * qzz
    exy, exz, eyz = 0.25 * qxy, 0.25 * qxz, 0.25 * qyz
    b_xy, b_xz, b_yz = half + (exx + eyy), half + (exx + ezz), half + (eyy + ezz)
    return {
        0: (6.0 * base, None),
        1: (base + 2.0 * exx, 2.0 * hx),
        3: (base + 2.0 * eyy, 2.0 * hy),
        5: (base + 2.0 * ezz, 2.0 * hz),
        7: (b_xy + exy, hx + hy),
        9: (b_xy - exy, hx - hy),
        11: (b_xz + exz, hx + hz),
        13: (b_xz - exz, hx - hz),
        15: (b_yz + eyz, hy + hz),
        17: (b_yz - eyz, hy - hz),
    }


def term_of(terms, pop):
    even, odd = terms[pop if pop % 2 else pop - 1]
    return even + odd if pop % 2 else even - odd


def kernel(
    pops_hbm, codes_hbm, cell_ref, vel_ref, spin_ref, rates_ref, coef_in,
    out, load_ref,
    f, codes, coef, post, parts, weights, split,
    state, message, arrived, table, loads, loads_in, scratch,
    in_sem, near_send, near_recv, load_send, load_recv,
):
    nx, ny = lax.axis_size("bx"), lax.axis_size("by")
    me_x, me_y = lax.axis_index("bx"), lax.axis_index("by")

    def device(t):
        dx, dy = NEAR[t]
        return (lax.rem(me_x + dx + nx, nx), lax.rem(me_y + dy + ny, ny))

    barrier = pltpu.get_barrier_semaphore()
    for t in SENDS:
        pl.semaphore_signal(barrier, inc=1, device_id=device(t), device_id_type=MESH)
    get_pops = pltpu.make_async_copy(pops_hbm, f, in_sem.at[1])
    get_pops.start()
    get_codes = pltpu.make_async_copy(codes_hbm, codes, in_sem.at[0])
    get_codes.start()

    lane = lax.broadcasted_iota(jnp.int32, (1, LANES), 1)
    sphere = lane & 3

    def along(values):
        return jnp.where(
            sphere < 2,
            jnp.where(sphere == 0, values[0], values[1]),
            jnp.where(sphere == 2, values[2], values[3]),
        )

    place = [cell_ref[0, 0, 0, k] + CX * cell_ref[1, 0, 0, k] for k in range(4)]
    rows = [along([v.astype(F32) for v in place])]
    rows.append(along([cell_ref[2, 0, 0, k].astype(F32) for k in range(4)]))
    for source in (vel_ref, spin_ref):
        for n in range(3):
            rows.append(along([source[n, 0, 0, k] for k in range(4)]))
    for n, row in enumerate(rows):
        state[n : n + 1, :] = row
    for t in SENDS:
        message[t, 0:8, :] = state[...]

    which = lax.broadcasted_iota(jnp.int32, (16, LANES), 0)
    rates = jnp.zeros((16, LANES), F32)
    for r in range(15):
        rates = jnp.where(which == r, rates_ref[r], rates)
    coef[...] = jnp.dot(
        coef_in[...], rates, precision=lax.Precision.HIGHEST, preferred_element_type=F32
    )

    lanes8 = lax.broadcasted_iota(jnp.int32, (CX, LANES), 1)
    rows8 = lax.broadcasted_iota(jnp.int32, (CX, LANES), 0)
    cell_x = rows8.astype(F32)
    cell_z = (lanes8 & (NZ - 1)).astype(F32)

    get_codes.wait()
    get_pops.wait()

    def fluid(chunk, carry):
        at = pl.ds(pl.multiple_of(chunk * LANES, LANES), LANES)
        p = [f[i, :, at] for i in range(19)]
        s = {a: p[a] + p[a + 1] for a in range(1, 19, 2)}
        d = {a: p[a] - p[a + 1] for a in range(1, 19, 2)}
        s_xy, a_xy = s[7] + s[9], s[7] - s[9]
        s_xz, a_xz = s[11] + s[13], s[11] - s[13]
        s_yz, a_yz = s[15] + s[17], s[15] - s[17]
        x1, x2 = d[7] + d[9], d[11] + d[13]
        y1, y2 = d[7] - d[9], d[15] + d[17]
        z1, z2 = d[11] - d[13], d[15] - d[17]
        density = (p[0] + s[1]) + (s[3] + s[5]) + (s_xy + s_xz) + s_yz
        jx, jy, jz = d[1] + x1 + x2, d[3] + y1 + y2, d[5] + z1 + z2
        inverse = 1.0 / density
        ux, uy, uz = jx * inverse, jy * inverse, jz * inverse
        code_of = [codes[layer, :, at] for layer in range(2)]
        cover = ((code_of[0] & 255) + (code_of[1] & 255)).astype(F32) * (1.0 / 255.0)

        my = ((lanes8 >> 6) + 2 * chunk).astype(F32)
        mz = cell_z - 32.0
        dx, dy, dz = density * cell_x, density * my, density * mz
        listed = (
            density, dx, dy, dz, dx * cell_x, dy * my, dz * mz, dx * my, dx * mz, dy * mz,
            jx, jy, jz, my * jz - mz * jy, mz * jx - cell_x * jz, cell_x * jy - my * jx,
        )
        for n, value in enumerate(listed):
            parts[chunk, CX * n : CX * (n + 1), :] = value

        keep = 1.0 - cover
        hx, hy, hz = 0.5 * jx * ux, 0.5 * jy * uy, 0.5 * jz * uz
        cxy, cxz, cyz = jx * uy, jx * uz, jy * uz
        base = density * (1.0 / 9.0) - (hx + hy + hz) * (1.0 / 3.0)
        e_x, e_y, e_z = base + hx, base + hy, base + hz
        e_xy, e_xz, e_yz = e_x + hy, e_x + hz, e_y + hz
        even = [s[1] - e_x, s[3] - e_y, s[5] - e_z, s_xy - e_xy, s_xz - e_xz, s_yz - e_yz]
        even = [keep * value for value in even]

        def c(n):
            return jnp.broadcast_to(coef[n : n + 1, :], (CX, LANES))

        sums = []
        for a in range(6):
            total = c(6 * a) * even[0]
            for b in range(1, 6):
                total = total + c(6 * a + b) * even[b]
            sums.append(total)
        third = 1.0 / 3.0
        odd = []
        for axis, (first, second, flow) in enumerate(((x1, x2, jx), (y1, y2, jy), (z1, z2, jz))):
            level = flow * third
            first, second = keep * (first - level), keep * (second - level)
            k = 36 + 4 * axis
            near = c(k) * first + c(k + 1) * second
            far = c(k + 2) * first + c(k + 3) * second
            odd.append((-2.0 * (near + far), near, far))
        n_xy = keep * (a_xy - cxy) * c(48)
        n_xz = keep * (a_xz - cxz) * c(49)
        n_yz = keep * (a_yz - cyz) * c(50)
        half, quarter = 0.5 * cover, 0.25 * cover
        gx, gy, gz = jx * (1.0 / 12.0), jy * (1.0 / 12.0), jz * (1.0 / 12.0)
        pairs = {
            1: (sums[0] + half * e_x, odd[0][0], 2.0 * gx),
            3: (sums[1] + half * e_y, odd[1][0], 2.0 * gy),
            5: (sums[2] + half * e_z, odd[2][0], 2.0 * gz),
            7: (sums[3] + n_xy + quarter * (e_xy + cxy), odd[0][1] + odd[1][1], gx + gy),
            9: (sums[3] - n_xy + quarter * (e_xy - cxy), odd[0][1] - odd[1][1], gx - gy),
            11: (sums[4] + n_xz + quarter * (e_xz + cxz), odd[0][2] + odd[2][1], gx + gz),
            13: (sums[4] - n_xz + quarter * (e_xz - cxz), odd[0][2] - odd[2][1], gx - gz),
            15: (sums[5] + n_yz + quarter * (e_yz + cyz), odd[1][2] + odd[2][2], gy + gz),
            17: (sums[5] - n_yz + quarter * (e_yz - cyz), odd[1][2] - odd[2][2], gy - gz),
        }
        rest = 2.0 * (sums[0] + sums[1] + sums[2]) + 4.0 * (sums[3] + sums[4] + sums[5])
        g = {0: p[0] + rest - 3.0 * cover * base}
        for a, (ev, od, flow) in pairs.items():
            od = od + cover * (d[a] - flow)
            g[a] = p[a] - ev - od
            g[a + 1] = p[a + 1] - ev + od
        for pop in range(19):
            post[pop, :, at] = g[pop]
        post[19, :, at] = density

        common = [density] + [value.astype(F32) for value in code_of]
        for row, names in ((CX - 1, X_UP), (0, X_DOWN)):
            t = NEAR.index((1 if row else -1, 0))
            for n, value in enumerate([g[pop] for pop in names] + common):
                message[t, pl.ds(8 + 8 * n + chunk, 1), :] = value[row : row + 1, :]
        return carry

    lax.fori_loop(0, CHUNKS, fluid, 0)

    codes_f = {c: [codes[layer, :, c * LANES : (c + 1) * LANES].astype(F32) for layer in range(2)] for c in (0, CHUNKS - 1)}
    for dy, names in ((1, Y_UP), (-1, Y_DOWN)):
        c = CHUNKS - 1 if dy > 0 else 0
        t = NEAR.index((0, dy))
        at = slice(c * LANES, (c + 1) * LANES)
        for n, value in enumerate([post[pop, :, at] for pop in (*names, 19)] + codes_f[c]):
            message[t, 8 + 8 * n : 16 + 8 * n, :] = value
    for pop, (sx, sy) in CORNERS.items():
        t = NEAR.index((-sx, -sy))
        row = CX - 1 if sx < 0 else 0
        c = CHUNKS - 1 if sy < 0 else 0
        at = slice(c * LANES, (c + 1) * LANES)
        for n, value in enumerate([post[pop, :, at], post[19, :, at]] + codes_f[c]):
            message[t, 8 + n : 9 + n, :] = value[row : row + 1, :]

    def length(t):
        dx, dy = NEAR[t]
        return 8 if abs(dx) == 2 else 16 if dx and dy else 72

    pl.semaphore_wait(barrier, 14)
    near = {}
    for n, t in enumerate(SENDS):
        there = 14 - t
        near[there] = pltpu.make_async_remote_copy(
            src_ref=message.at[t, 0 : length(t)], dst_ref=arrived.at[there, 0 : length(t)],
            send_sem=near_send.at[n], recv_sem=near_recv.at[there],
            device_id=device(t), device_id_type=MESH,
        )
        near[there].start()

    slot_rows = lax.broadcasted_iota(jnp.int32, (ROWS, CELLS), 0)

    def fill(row, carry):
        total = None
        for layer in range(2):
            packed = codes[layer, pl.ds(row, 1), :]
            level = (packed & 255).astype(F32)
            hit = jnp.where((packed >> 8) == slot_rows, level, 0.0)
            total = hit if total is None else total + hit
        weights[:, pl.ds(pl.multiple_of(row * CELLS, CELLS), CELLS)] = total.astype(jnp.bfloat16)
        return carry

    lax.fori_loop(0, CX, fill, 0)

    def halves(chunk, carry):
        for row in range(CX):
            value = parts[chunk, pl.ds(row, MOMENTS, stride=CX), :]
            high = value.astype(jnp.bfloat16).astype(F32)
            both = jnp.concatenate([high, value - high], axis=0)
            at = pl.multiple_of(row * CELLS + chunk * LANES, LANES)
            split[:, pl.ds(at, LANES)] = both.astype(jnp.bfloat16)
        return carry

    lax.fori_loop(0, CHUNKS, halves, 0)
    sums = lax.dot_general(
        split[...], weights[...], (((1,), (1,)), ((), ())), preferred_element_type=F32
    )
    loads[...] = jnp.zeros_like(loads)
    loads[:, 0:ROWS] = sums[0:MOMENTS] + sums[MOMENTS : 2 * MOMENTS]
    beside = {}
    for n, t in enumerate(BESIDE):
        there = 14 - t
        beside[there] = pltpu.make_async_remote_copy(
            src_ref=loads, dst_ref=loads_in.at[there],
            send_sem=load_send.at[n], recv_sem=load_recv.at[there],
            device_id=device(t), device_id_type=MESH,
        )
        beside[there].start()

    for t in SENDS:
        near[t].wait()
    group = (lanes8 - 4) >> 2
    full = jnp.where(group == HERE, state[...], 0.0)
    for t in SENDS:
        full = jnp.where(group == t, arrived[t, 0:8, :], full)
    place = full[0:1].astype(jnp.int32)
    group = group[0:1]
    group_x = (
        (group >= 3).astype(jnp.int32) + (group >= 6).astype(jnp.int32)
        + (group >= 9).astype(jnp.int32) + (group >= 12).astype(jnp.int32)
    )
    table[0:1, :] = ((place & (CX - 1)) + (group_x - 2) * CX).astype(F32)
    table[1:2, :] = ((place >> 3) + (group - 3 * group_x - 1) * CY).astype(F32)
    table[2:9, :] = full[1:8]

    def covers(chunk, carry):
        at = pl.ds(pl.multiple_of(chunk * LANES, LANES), LANES)
        cell_y = ((lanes8 >> 6) + 2 * chunk).astype(F32)
        terms = sphere_terms(
            post[19, :, at], [codes[layer, :, at] for layer in range(2)], table,
            (cell_x, cell_y, cell_z), 4 + 4 * 3,
        )
        post[0, :, at] = post[0, :, at] + terms[0][0]
        for pop in range(1, 19):
            post[pop, :, at] = post[pop, :, at] + term_of(terms, pop)
        return carry

    lax.fori_loop(0, CHUNKS, covers, 0)

    lower = lanes8 < NZ
    halo_x = {}
    for side, names in ((0, X_UP), (1, X_DOWN)):
        t = NEAR.index((-1 if side == 0 else 1, 0))
        got = [arrived[t, 8 + 8 * n : 16 + 8 * n, :] for n in range(8)]
        cells = (
            jnp.full((CX, LANES), -1.0 if side == 0 else float(CX), F32),
            (2 * rows8 + (lanes8 >> 6)).astype(F32),
            cell_z,
        )
        terms = sphere_terms(
            got[5], [v.astype(jnp.int32) for v in got[6:8]], table, cells, 16 + (-12 if side == 0 else 12)
        )
        for n, pop in enumerate(names):
            value = got[n] + term_of(terms, pop)
            shift = lane_shift(pop) % LANES
            if shift:
                value = pltpu.roll(value, shift, 1)
            step_y = int(VELOCITIES[pop, 1])
            if step_y:
                crossed = lower if step_y > 0 else jnp.logical_not(lower)
                value = jnp.where(crossed, pltpu.roll(value, step_y % CX, 0), value)
            halo_x[pop] = value
    from_low, from_high = NEAR.index((0, -1)), NEAR.index((0, 1))
    got_low = [arrived[from_low, 8 + 8 * n : 16 + 8 * n, :] for n in range(8)]
    got_high = [arrived[from_high, 8 + 8 * n : 16 + 8 * n, :] for n in range(8)]
    mixed = [jnp.where(lower, got_high[n], got_low[n]) for n in range(5, 8)]
    cells = (cell_x, jnp.where(lower, float(CY), -1.0), cell_z)
    terms = sphere_terms(
        mixed[0], [v.astype(jnp.int32) for v in mixed[1:]], table, cells, jnp.where(lower, 20, 12)
    )
    halo_y = {}
    for names, got in ((Y_UP, got_low), (Y_DOWN, got_high)):
        for n, pop in enumerate(names):
            value = got[n] + term_of(terms, pop)
            value = pltpu.roll(value, lane_shift(pop) % LANES, 1)
            step_x = int(VELOCITIES[pop, 0])
            if step_x:
                value = pltpu.roll(value, step_x % CX, 0)
            halo_y[pop] = value
    corner = [jnp.zeros((CX, LANES), F32) for _ in range(4)]
    corner_x = corner_y = jnp.zeros((CX, LANES), F32)
    corner_slot = jnp.zeros((CX, LANES), jnp.int32)
    for row, (pop, (sx, sy)) in enumerate(CORNERS.items()):
        t = NEAR.index((sx, sy))
        here = rows8 == row
        for n in range(4):
            piece = jnp.broadcast_to(arrived[t, 8 + n : 9 + n, :], (CX, LANES))
            corner[n] = jnp.where(here, piece, corner[n])
        corner_x = jnp.where(here, -1.0 if sx < 0 else float(CX), corner_x)
        corner_y = jnp.where(here, -1.0 if sy < 0 else float(CY), corner_y)
        corner_slot = jnp.where(here, 16 + 12 * sx + 4 * sy, corner_slot)
    terms = sphere_terms(
        corner[1], [v.astype(jnp.int32) for v in corner[2:4]], table, (corner_x, corner_y, cell_z), corner_slot
    )
    corner_term = jnp.zeros((CX, LANES), F32)
    for row, pop in enumerate(CORNERS):
        corner_term = jnp.where(rows8 == row, term_of(terms, pop), corner_term)
    corner_of = pltpu.roll(corner[0] + corner_term, NZ, 1)

    z_of = lax.broadcasted_iota(jnp.int32, (CX, CELLS), 1) & (NZ - 1)
    edge = {1: z_of == 0, -1: z_of == NZ - 1}
    row_of = lax.broadcasted_iota(jnp.int32, (CX, CELLS), 0)
    for n, pop in enumerate((*X_UP, *X_DOWN)):
        scratch[n] = halo_x[pop]
    for pop in range(19):
        step_x, step_y, step_z = (int(v) for v in VELOCITIES[pop])
        value = post[pop]
        shift = lane_shift(pop) % CELLS
        if shift:
            value = pltpu.roll(value, shift, 1)
        if step_x:
            value = pltpu.roll(value, step_x % CX, 0)
            row = 0 if step_x > 0 else CX - 1
            n = (*X_UP, *X_DOWN).index(pop)
            beside_x = jnp.concatenate(
                [jnp.broadcast_to(scratch[n, c : c + 1, :], (CX, LANES)) for c in range(CHUNKS)], axis=1
            )
            value = jnp.where(row_of == row, beside_x, value)
        if step_y:
            tile = halo_y[pop]
            if step_x:
                k = list(CORNERS).index(pop)
                tile = jnp.where(rows8 == row, jnp.broadcast_to(corner_of[k : k + 1], (CX, LANES)), tile)
            if step_y > 0:
                value = jnp.concatenate([jnp.where(lower, tile, value[:, :LANES]), value[:, LANES:]], axis=1)
            else:
                value = jnp.concatenate([value[:, :-LANES], jnp.where(lower, value[:, -LANES:], tile)], axis=1)
        if step_z:
            value = jnp.where(edge[step_z], post[OPPOSITE[pop]], value)
        out[pop] = value

    for t in BESIDE:
        beside[t].wait()
    lanes16 = lax.broadcasted_iota(jnp.int32, (MOMENTS, LANES), 1) >> 2
    moment = jnp.where(lanes16 == 4, loads[...], 0.0)
    for t in BESIDE:
        dx, dy = NEAR[t]
        moment = jnp.where(lanes16 == (1 - dx) * 3 + 1 - dy, loads_in[t], moment)
    m = [moment[n : n + 1, :] for n in range(MOMENTS)]
    group = lane >> 2
    group_x = (group >= 3).astype(jnp.int32) + (group >= 6).astype(jnp.int32)
    place = state[0:1, :].astype(jnp.int32)
    cx = ((place & (CX - 1)) + (group_x - 1) * CX).astype(F32)
    cy = ((place >> 3) + (group - 3 * group_x - 1) * CY).astype(F32)
    cz = state[1:2, :] - 32.0
    vx, vy, vz, sx, sy, sz = [state[n : n + 1, :] for n in range(2, 8)]
    ex, ey, ez = m[1] - cx * m[0], m[2] - cy * m[0], m[3] - cz * m[0]
    qxx = m[4] - cx * (m[1] + ex)
    qyy = m[5] - cy * (m[2] + ey)
    qzz = m[6] - cz * (m[3] + ez)
    qxy = m[7] - cx * m[2] - cy * ex
    qxz = m[8] - cx * m[3] - cz * ex
    qyz = m[9] - cy * m[3] - cz * ey
    fx = m[10] - vx * m[0] - (sy * ez - sz * ey)
    fy = m[11] - vy * m[0] - (sz * ex - sx * ez)
    fz = m[12] - vz * m[0] - (sx * ey - sy * ex)
    tx = m[13] - (cy * m[12] - cz * m[11]) - (ey * vz - ez * vy) - (sx * (qyy + qzz) - sy * qxy - sz * qxz)
    ty = m[14] - (cz * m[10] - cx * m[12]) - (ez * vx - ex * vz) - (sy * (qxx + qzz) - sx * qxy - sz * qyz)
    tz = m[15] - (cx * m[11] - cy * m[10]) - (ex * vy - ey * vx) - (sz * (qxx + qyy) - sx * qxz - sy * qyz)
    force, torque = 1.0 / (255.0 * RADIUS**2), 1.0 / (255.0 * RADIUS**3)
    listed = (fx * force, fy * force, fz * force, tx * torque, ty * torque, tz * torque)
    tile = jnp.zeros((CX, LANES), F32)
    for n, value in enumerate(listed):
        tile = jnp.where(rows8 == n, jnp.broadcast_to(value, (CX, LANES)), tile)
    tile = jnp.where(lanes8 < 36, tile, 0.0)
    total = tile
    for g in range(1, 9):
        total = total + pltpu.roll(tile, LANES - 4 * g, 1)
    load_ref[...] = total.T[0:4, 0:6]


def per_device(populations, cover_codes, sphere_cell, sphere_velocity, sphere_spin, relax_rates):
    vmem, smem, anywhere = (
        pl.BlockSpec(memory_space=pltpu.VMEM),
        pl.BlockSpec(memory_space=pltpu.SMEM),
        pl.BlockSpec(memory_space=pl.ANY),
    )
    dma = pltpu.SemaphoreType.DMA
    out, load = pl.pallas_call(
        kernel,
        out_shape=(
            pltpu.VMEM((19, CX, CELLS), F32),
            jax.ShapeDtypeStruct((4, 6), F32),
        ),
        in_specs=[anywhere, anywhere, smem, smem, smem, smem, vmem],
        out_specs=(vmem, vmem),
        scratch_shapes=[
            pltpu.VMEM((19, CX, CELLS), F32),
            pltpu.VMEM((2, CX, CELLS), jnp.int32),
            pltpu.VMEM((64, LANES), F32),
            pltpu.VMEM((20, CX, CELLS), F32),
            pltpu.VMEM((CHUNKS, MOMENTS * CX, LANES), F32),
            pltpu.VMEM((ROWS, CX * CELLS), jnp.bfloat16),
            pltpu.VMEM((2 * MOMENTS, CX * CELLS), jnp.bfloat16),
            pltpu.VMEM((8, LANES), F32),
            pltpu.VMEM((15, 72, LANES), F32),
            pltpu.VMEM((15, 72, LANES), F32),
            pltpu.VMEM((16, LANES), F32),
            pltpu.VMEM((MOMENTS, LANES), F32),
            pltpu.VMEM((15, MOMENTS, LANES), F32),
            pltpu.VMEM((10, CX, LANES), F32),
            dma((2,)),
            dma((14,)),
            dma((15,)),
            dma((8,)),
            dma((15,)),
        ],
        compiler_params=pltpu.CompilerParams(
            collective_id=0, has_side_effects=True, vmem_limit_bytes=60 * 1024 * 1024
        ),
    )(
        populations, cover_codes, sphere_cell, sphere_velocity, sphere_spin, relax_rates,
        jnp.asarray(coefficient_rows()),
    )
    return out, load.T.reshape(6, 1, 1, 4)


def solution(mesh):
    placed = (
        P(None, "bx", "by"),
        P(None, "bx", "by"),
        P(None, "bx", "by", None),
        P(None, "bx", "by", None),
        P(None, "bx", "by", None),
        P(),
    )
    return jax.shard_map(
        per_device,
        mesh=mesh,
        in_specs=placed,
        out_specs=(P(None, "bx", "by"), P(None, "bx", "by", None)),
        check_vma=False,
    )
```

time: 37.4 us -> 31.7 us (0.85)
  Pallas kernels: 35.1 us -> 29.4 us
    pallas_call x1, Pallas kernels: 35.1 us -> 29.4 us  [per_device(): pl.pallas_call(kernel, out_shape=(pltpu.VMEM((19, CX, CELLS), F32), jax.S...]
where the time goes in v3:
time: 31.7 us; the launch traced here: 31.5 us
  Pallas kernels  29.4 us (93%)
  local copies, waits for them, and re-layouts  1.41 us (4%)
  between operations  0.65 us (2%)
    pallas_call x1, Pallas kernels, per_device(): pl.pallas_call(kernel, out_shape=(pltpu.VMEM((19, CX, CELLS), F32), jax.S...  29.4 us
    unnamed x4, local copies, waits for them, and re-layouts  1.41 us

profile of v3, /device:TPU:1, one launch (start us, length us, event | category | flops | bytes accessed | tf_op | source)
XLA Modules:
  0.0 31.5 jit_solution(3076180745923285012)
XLA Ops:
  0.6 29.4 %shard_map.86 = (f32[19,8,1024]{2,1,0:T(8,128)S(1)}, f32[4,6]{1,0:T(4,128)}) custom-call(f32[19,8,1024]{2,1,0:T(8,128)} %pops_hbm.1, s32[2,8,1024]{2,1,0:T(8,128)} %codes_hbm.1, s32[3,1,1,4]{3,2,1,0:T(1,128)} %cell_ref.1, f32[3,1,1,4]{3,2,1,0:T(1,128)} %vel_ref.1, f32[3,1,1,4]{3,2,1,0:T(1,128)} %spin_ref.1, f32[15]{0:T(128)} %rates_ref.1, ...), custom_call_target="tpu_custom_call" | custom-call | tf_op jit(solution)/shard_map/pallas_call | solution.py:547
  30.0 0.0 copy-start
  30.1 0.8 %copy.11 = f32[19,8,1024]{2,1,0:T(8,128)} copy(f32[19,8,1024]{2,1,0:T(8,128)S(1)} %get-tuple-element.6) | data formatting | bytes 1245184
  30.9 0.0 copy-done
  30.9 0.6 %copy.12 = f32[6,1,1,4]{0,3,2,1:T(4,128)} copy(f32[6,1,1,4]{0,3,2,1:T(4,128)S(1)} %bitcast.3) | data formatting | bytes 192
Async XLA Ops:
  30.0 0.8 %copy-start = (f32[4,6]{1,0:T(4,128)S(1)}, f32[4,6]{1,0:T(4,128)}, u32[]{:S(2)}) copy-start(f32[4,6]{1,0:T(4,128)} %get-tuple-element.5) | copy-start | bytes 292

commit v4 on v3

--- a/solution.py
+++ b/solution.py
@@ -158,10 +158,10 @@
 
 
 def kernel(
-    pops_hbm, codes_hbm, cell_ref, vel_ref, spin_ref, rates_ref, coef_in,
-    out, load_ref,
-    f, codes, coef, post, parts, weights, split,
-    state, message, arrived, table, loads, loads_in, scratch,
+    pops_hbm, codes_hbm, cell_hbm, vel_hbm, spin_hbm, rates_hbm, coef_hbm,
+    post, halo, corner_out, load_ref,
+    cell_ref, vel_ref, spin_ref, rates_ref, coef_in, f, codes, coef, parts, weights, split,
+    state, message, arrived, table, loads, loads_in,
     in_sem, near_send, near_recv, load_send, load_recv,
 ):
     nx, ny = lax.axis_size("bx"), lax.axis_size("by")
@@ -174,10 +174,15 @@
     barrier = pltpu.get_barrier_semaphore()
     for t in SENDS:
         pl.semaphore_signal(barrier, inc=1, device_id=device(t), device_id_type=MESH)
-    get_pops = pltpu.make_async_copy(pops_hbm, f, in_sem.at[1])
-    get_pops.start()
-    get_codes = pltpu.make_async_copy(codes_hbm, codes, in_sem.at[0])
-    get_codes.start()
+    fetched = []
+    for n, (src, dst) in enumerate(
+        (
+            (cell_hbm, cell_ref), (vel_hbm, vel_ref), (spin_hbm, spin_ref), (rates_hbm, rates_ref),
+            (coef_hbm, coef_in), (codes_hbm, codes), (pops_hbm, f),
+        )
+    ):
+        fetched.append(pltpu.make_async_copy(src, dst, in_sem.at[n]))
+        fetched[-1].start()
 
     lane = lax.broadcasted_iota(jnp.int32, (1, LANES), 1)
     sphere = lane & 3
@@ -189,6 +194,8 @@
             jnp.where(sphere == 2, values[2], values[3]),
         )
 
+    for copy in fetched[:5]:
+        copy.wait()
     place = [cell_ref[0, 0, 0, k] + CX * cell_ref[1, 0, 0, k] for k in range(4)]
     rows = [along([v.astype(F32) for v in place])]
     rows.append(along([cell_ref[2, 0, 0, k].astype(F32) for k in range(4)]))
@@ -213,8 +220,21 @@
     cell_x = rows8.astype(F32)
     cell_z = (lanes8 & (NZ - 1)).astype(F32)
 
-    get_codes.wait()
-    get_pops.wait()
+    fetched[5].wait()
+    slot_rows = lax.broadcasted_iota(jnp.int32, (ROWS, CELLS), 0)
+
+    def fill(row, carry):
+        total = None
+        for layer in range(2):
+            packed = codes[layer, pl.ds(row, 1), :]
+            level = (packed & 255).astype(F32)
+            hit = jnp.where((packed >> 8) == slot_rows, level, 0.0)
+            total = hit if total is None else total + hit
+        weights[:, pl.ds(pl.multiple_of(row * CELLS, CELLS), CELLS)] = total.astype(jnp.bfloat16)
+        return carry
+
+    lax.fori_loop(0, CX, fill, 0, unroll=8)
+    fetched[6].wait()
 
     def fluid(chunk, carry):
         at = pl.ds(pl.multiple_of(chunk * LANES, LANES), LANES)
@@ -304,7 +324,7 @@
                 message[t, pl.ds(8 + 8 * n + chunk, 1), :] = value[row : row + 1, :]
         return carry
 
-    lax.fori_loop(0, CHUNKS, fluid, 0)
+    lax.fori_loop(0, CHUNKS, fluid, 0, unroll=8)
 
     codes_f = {c: [codes[layer, :, c * LANES : (c + 1) * LANES].astype(F32) for layer in range(2)] for c in (0, CHUNKS - 1)}
     for dy, names in ((1, Y_UP), (-1, Y_DOWN)):
@@ -336,20 +356,6 @@
         )
         near[there].start()
 
-    slot_rows = lax.broadcasted_iota(jnp.int32, (ROWS, CELLS), 0)
-
-    def fill(row, carry):
-        total = None
-        for layer in range(2):
-            packed = codes[layer, pl.ds(row, 1), :]
-            level = (packed & 255).astype(F32)
-            hit = jnp.where((packed >> 8) == slot_rows, level, 0.0)
-            total = hit if total is None else total + hit
-        weights[:, pl.ds(pl.multiple_of(row * CELLS, CELLS), CELLS)] = total.astype(jnp.bfloat16)
-        return carry
-
-    lax.fori_loop(0, CX, fill, 0)
-
     def halves(chunk, carry):
         for row in range(CX):
             value = parts[chunk, pl.ds(row, MOMENTS, stride=CX), :]
@@ -359,7 +365,7 @@
             split[:, pl.ds(at, LANES)] = both.astype(jnp.bfloat16)
         return carry
 
-    lax.fori_loop(0, CHUNKS, halves, 0)
+    lax.fori_loop(0, CHUNKS, halves, 0, unroll=8)
     sums = lax.dot_general(
         split[...], weights[...], (((1,), (1,)), ((), ())), preferred_element_type=F32
     )
@@ -403,7 +409,7 @@
             post[pop, :, at] = post[pop, :, at] + term_of(terms, pop)
         return carry
 
-    lax.fori_loop(0, CHUNKS, covers, 0)
+    lax.fori_loop(0, CHUNKS, covers, 0, unroll=8)
 
     lower = lanes8 < NZ
     halo_x = {}
@@ -465,37 +471,11 @@
         corner_term = jnp.where(rows8 == row, term_of(terms, pop), corner_term)
     corner_of = pltpu.roll(corner[0] + corner_term, NZ, 1)
 
-    z_of = lax.broadcasted_iota(jnp.int32, (CX, CELLS), 1) & (NZ - 1)
-    edge = {1: z_of == 0, -1: z_of == NZ - 1}
-    row_of = lax.broadcasted_iota(jnp.int32, (CX, CELLS), 0)
     for n, pop in enumerate((*X_UP, *X_DOWN)):
-        scratch[n] = halo_x[pop]
-    for pop in range(19):
-        step_x, step_y, step_z = (int(v) for v in VELOCITIES[pop])
-        value = post[pop]
-        shift = lane_shift(pop) % CELLS
-        if shift:
-            value = pltpu.roll(value, shift, 1)
-        if step_x:
-            value = pltpu.roll(value, step_x % CX, 0)
-            row = 0 if step_x > 0 else CX - 1
-            n = (*X_UP, *X_DOWN).index(pop)
-            beside_x = jnp.concatenate(
-                [jnp.broadcast_to(scratch[n, c : c + 1, :], (CX, LANES)) for c in range(CHUNKS)], axis=1
-            )
-            value = jnp.where(row_of == row, beside_x, value)
-        if step_y:
-            tile = halo_y[pop]
-            if step_x:
-                k = list(CORNERS).index(pop)
-                tile = jnp.where(rows8 == row, jnp.broadcast_to(corner_of[k : k + 1], (CX, LANES)), tile)
-            if step_y > 0:
-                value = jnp.concatenate([jnp.where(lower, tile, value[:, :LANES]), value[:, LANES:]], axis=1)
-            else:
-                value = jnp.concatenate([value[:, :-LANES], jnp.where(lower, value[:, -LANES:], tile)], axis=1)
-        if step_z:
-            value = jnp.where(edge[step_z], post[OPPOSITE[pop]], value)
-        out[pop] = value
+        halo[0, n] = halo_x[pop]
+    for n, pop in enumerate((*Y_UP, *Y_DOWN)):
+        halo[1, n] = halo_y[pop]
+    corner_out[...] = corner_of
 
     for t in BESIDE:
         beside[t].wait()
@@ -537,26 +517,71 @@
     load_ref[...] = total.T[0:4, 0:6]
 
 
+def finish(post, halo, corner_of, load, out_hbm, load_hbm, out, out_sem):
+    put_load = pltpu.make_async_copy(load, load_hbm, out_sem.at[19])
+    put_load.start()
+    puts = []
+    lanes8 = lax.broadcasted_iota(jnp.int32, (CX, LANES), 1)
+    rows8 = lax.broadcasted_iota(jnp.int32, (CX, LANES), 0)
+    lower = lanes8 < NZ
+    z_of = lax.broadcasted_iota(jnp.int32, (CX, CELLS), 1) & (NZ - 1)
+    edge = {1: z_of == 0, -1: z_of == NZ - 1}
+    row_of = lax.broadcasted_iota(jnp.int32, (CX, CELLS), 0)
+    for pop in range(19):
+        step_x, step_y, step_z = (int(v) for v in VELOCITIES[pop])
+        value = post[pop]
+        shift = lane_shift(pop) % CELLS
+        if shift:
+            value = pltpu.roll(value, shift, 1)
+        if step_x:
+            value = pltpu.roll(value, step_x % CX, 0)
+            row = 0 if step_x > 0 else CX - 1
+            n = (*X_UP, *X_DOWN).index(pop)
+            beside_x = jnp.concatenate(
+                [jnp.broadcast_to(halo[0, n, c : c + 1, :], (CX, LANES)) for c in range(CHUNKS)], axis=1
+            )
+            value = jnp.where(row_of == row, beside_x, value)
+        if step_y:
+            tile = halo[1, (*Y_UP, *Y_DOWN).index(pop)]
+            if step_x:
+                k = list(CORNERS).index(pop)
+                tile = jnp.where(rows8 == row, jnp.broadcast_to(corner_of[k : k + 1, :], (CX, LANES)), tile)
+            if step_y > 0:
+                value = jnp.concatenate([jnp.where(lower, tile, value[:, :LANES]), value[:, LANES:]], axis=1)
+            else:
+                value = jnp.concatenate([value[:, :-LANES], jnp.where(lower, value[:, -LANES:], tile)], axis=1)
+        if step_z:
+            value = jnp.where(edge[step_z], post[OPPOSITE[pop]], value)
+        out[pop] = value
+        puts.append(pltpu.make_async_copy(out.at[pop], out_hbm.at[pop], out_sem.at[pop]))
+        puts[-1].start()
+    put_load.wait()
+    for put in puts:
+        put.wait()
+
+
 def per_device(populations, cover_codes, sphere_cell, sphere_velocity, sphere_spin, relax_rates):
-    vmem, smem, anywhere = (
-        pl.BlockSpec(memory_space=pltpu.VMEM),
-        pl.BlockSpec(memory_space=pltpu.SMEM),
-        pl.BlockSpec(memory_space=pl.ANY),
-    )
+    vmem, anywhere = pl.BlockSpec(memory_space=pltpu.VMEM), pl.BlockSpec(memory_space=pl.ANY)
     dma = pltpu.SemaphoreType.DMA
-    out, load = pl.pallas_call(
+    post, halo, corner, load = pl.pallas_call(
         kernel,
         out_shape=(
-            pltpu.VMEM((19, CX, CELLS), F32),
-            jax.ShapeDtypeStruct((4, 6), F32),
+            pltpu.VMEM((20, CX, CELLS), F32),
+            pltpu.VMEM((2, 10, CX, LANES), F32),
+            pltpu.VMEM((CX, LANES), F32),
+            pltpu.VMEM((4, 6), F32),
         ),
-        in_specs=[anywhere, anywhere, smem, smem, smem, smem, vmem],
-        out_specs=(vmem, vmem),
+        in_specs=[anywhere] * 7,
+        out_specs=(vmem,) * 4,
         scratch_shapes=[
+            pltpu.SMEM((3, 1, 1, 4), jnp.int32),
+            pltpu.SMEM((3, 1, 1, 4), F32),
+            pltpu.SMEM((3, 1, 1, 4), F32),
+            pltpu.SMEM((15,), F32),
+            pltpu.VMEM((64, 16), F32),
             pltpu.VMEM((19, CX, CELLS), F32),
             pltpu.VMEM((2, CX, CELLS), jnp.int32),
             pltpu.VMEM((64, LANES), F32),
-            pltpu.VMEM((20, CX, CELLS), F32),
             pltpu.VMEM((CHUNKS, MOMENTS * CX, LANES), F32),
             pltpu.VMEM((ROWS, CX * CELLS), jnp.bfloat16),
             pltpu.VMEM((2 * MOMENTS, CX * CELLS), jnp.bfloat16),
@@ -566,8 +591,7 @@
             pltpu.VMEM((16, LANES), F32),
             pltpu.VMEM((MOMENTS, LANES), F32),
             pltpu.VMEM((15, MOMENTS, LANES), F32),
-            pltpu.VMEM((10, CX, LANES), F32),
-            dma((2,)),
+            dma((7,)),
             dma((14,)),
             dma((15,)),
             dma((8,)),
@@ -580,6 +604,14 @@
         populations, cover_codes, sphere_cell, sphere_velocity, sphere_spin, relax_rates,
         jnp.asarray(coefficient_rows()),
     )
+    out, load = pl.pallas_call(
+        finish,
+        out_shape=(jax.ShapeDtypeStruct((19, CX, CELLS), F32), jax.ShapeDtypeStruct((4, 6), F32)),
+        in_specs=[vmem] * 4,
+        out_specs=(anywhere, anywhere),
+        scratch_shapes=[pltpu.VMEM((19, CX, CELLS), F32), dma((20,))],
+        compiler_params=pltpu.CompilerParams(vmem_limit_bytes=8 * 1024 * 1024),
+    )(*[pltpu.with_memory_space_constraint(v, pltpu.VMEM) for v in (post, halo, corner, load)])
     return out, load.T.reshape(6, 1, 1, 4)
 
 

time: 31.7 us -> 29.2 us (0.921)
  local copies, waits for them, and re-layouts: 1.41 us -> 0 us
  Pallas kernels: 29.4 us -> 28.4 us
    unnamed x4 -> x0, local copies, waits for them, and re-layouts: 1.41 us -> none
    pallas_call x1 -> x2, Pallas kernels: 29.4 us -> 28.4 us  [the longest x1 27.4 us: per_device(): pl.pallas_call(kernel, out_shape=(pltpu.VMEM((20, CX, CELLS), F32), pltpu...]
where the time goes in v4:
time: 29.2 us; the launch traced here: 29 us
  Pallas kernels  28.4 us (97%)
  between operations  0.64 us (2%)
    pallas_call x1, Pallas kernels, per_device(): pl.pallas_call(kernel, out_shape=(pltpu.VMEM((20, CX, CELLS), F32), pltpu...  27.4 us
    pallas_call x1, Pallas kernels, per_device(): pl.pallas_call(finish, out_shape=(jax.ShapeDtypeStruct((19, CX, CELLS), F...  1.03 us

profile of v4, /device:TPU:1, one launch (start us, length us, event | category | flops | bytes accessed | tf_op | source)
XLA Modules:
  0.0 29.0 jit_solution(14315606645696398320)
XLA Ops:
  0.6 27.4 %shard_map.86 = (f32[20,8,1024]{2,1,0:T(8,128)S(1)}, f32[2,10,8,128]{3,2,1,0:T(8,128)S(1)}, f32[8,128]{1,0:T(8,128)S(1)}, f32[4,6]{1,0:T(4,128)S(1)}) custom-call(f32[19,8,1024]{2,1,0:T(8,128)} %pops_hbm.1, s32[2,8,1024]{2,1,0:T(8,128)} %codes_hbm.1, s32[3,1,1,4]{3,2,1,0:T(1,128)} %cell_hbm.1, f32[3,1,1,4]{3,2,1,0:T(1,128)} %vel_hbm.1, ...), custom_call_target="tpu_custom_call" | custom-call | tf_op jit(solution)/shard_map/pallas_call | solution.py:566
  28.0 1.0 %shard_map.87 = (f32[19,8,1024]{2,1,0:T(8,128)}, f32[4,6]{1,0:T(4,128)}) custom-call(f32[20,8,1024]{2,1,0:T(8,128)S(1)} %get-tuple-element.8.post, f32[2,10,8,128]{3,2,1,0:T(8,128)S(1)} %get-tuple-element.9.halo, f32[8,128]{1,0:T(8,128)S(1)} %get-tuple-element.10.corner_of, f32[4,6]{1,0:T(4,128)S(1)} %get-tuple-element.11.load), custom_call_target="tpu_custom_call" | custom-call | tf_op jit(solution)/shard_map/pallas_call | solution.py:607

commit v5 on v4

--- a/solution.py
+++ b/solution.py
@@ -109,14 +109,14 @@
 def sphere_terms(density, codes, table, cell, first_slot):
     flow, square, cover = None, None, None
     for packed in codes:
-        slot = (packed >> 8) + first_slot
+        slot = ((packed >> 8) + first_slot) & 63
         weight = (packed & 255).astype(F32) * (1.0 / 255.0) * density
         got = [
             jnp.take_along_axis(
-                jnp.broadcast_to(table[n : n + 1, :], (CX, LANES)), slot,
+                jnp.broadcast_to(table[n : n + 1, :], (CX, LANES)), at,
                 axis=1, mode="promise_in_bounds",
             )
-            for n in range(9)
+            for n, at in ((0, slot), (0, slot + 64), *((n, slot) for n in range(1, 8)))
         ]
         rx, ry, rz = cell[0] - got[0], cell[1] - got[1], cell[2] - got[2]
         wx = got[3] + got[7] * rz - got[8] * ry
@@ -161,8 +161,8 @@
     pops_hbm, codes_hbm, cell_hbm, vel_hbm, spin_hbm, rates_hbm, coef_hbm,
     post, halo, corner_out, load_ref,
     cell_ref, vel_ref, spin_ref, rates_ref, coef_in, f, codes, coef, parts, weights, split,
-    state, message, arrived, table, loads, loads_in,
-    in_sem, near_send, near_recv, load_send, load_recv,
+    state, message, arrived, table, loads,
+    in_sem, near_send, near_recv,
 ):
     nx, ny = lax.axis_size("bx"), lax.axis_size("by")
     me_x, me_y = lax.axis_index("bx"), lax.axis_index("by")
@@ -196,9 +196,8 @@
 
     for copy in fetched[:5]:
         copy.wait()
-    place = [cell_ref[0, 0, 0, k] + CX * cell_ref[1, 0, 0, k] for k in range(4)]
-    rows = [along([v.astype(F32) for v in place])]
-    rows.append(along([cell_ref[2, 0, 0, k].astype(F32) for k in range(4)]))
+    place = [along([cell_ref[n, 0, 0, k].astype(F32) for k in range(4)]) for n in range(3)]
+    rows = [jnp.where(lane < NZ, place[0], place[1]), place[2]]
     for source in (vel_ref, spin_ref):
         for n in range(3):
             rows.append(along([source[n, 0, 0, k] for k in range(4)]))
@@ -321,7 +320,7 @@
         for row, names in ((CX - 1, X_UP), (0, X_DOWN)):
             t = NEAR.index((1 if row else -1, 0))
             for n, value in enumerate([g[pop] for pop in names] + common):
-                message[t, pl.ds(8 + 8 * n + chunk, 1), :] = value[row : row + 1, :]
+                message[t, pl.ds(16 + 8 * n + chunk, 1), :] = value[row : row + 1, :]
         return carry
 
     lax.fori_loop(0, CHUNKS, fluid, 0, unroll=8)
@@ -332,18 +331,38 @@
         t = NEAR.index((0, dy))
         at = slice(c * LANES, (c + 1) * LANES)
         for n, value in enumerate([post[pop, :, at] for pop in (*names, 19)] + codes_f[c]):
-            message[t, 8 + 8 * n : 16 + 8 * n, :] = value
+            message[t, 16 + 8 * n : 24 + 8 * n, :] = value
     for pop, (sx, sy) in CORNERS.items():
         t = NEAR.index((-sx, -sy))
         row = CX - 1 if sx < 0 else 0
         c = CHUNKS - 1 if sy < 0 else 0
         at = slice(c * LANES, (c + 1) * LANES)
         for n, value in enumerate([post[pop, :, at], post[19, :, at]] + codes_f[c]):
-            message[t, 8 + n : 9 + n, :] = value[row : row + 1, :]
+            message[t, 16 + n : 17 + n, :] = value[row : row + 1, :]
+
+    def halves(chunk, carry):
+        for row in range(CX):
+            value = parts[chunk, pl.ds(row, MOMENTS, stride=CX), :]
+            high = value.astype(jnp.bfloat16).astype(F32)
+            both = jnp.concatenate([high, value - high], axis=0)
+            at = pl.multiple_of(row * CELLS + chunk * LANES, LANES)
+            split[:, pl.ds(at, LANES)] = both.astype(jnp.bfloat16)
+        return carry
+
+    lax.fori_loop(0, CHUNKS, halves, 0, unroll=8)
+    sums = lax.dot_general(
+        split[...], weights[...], (((1,), (1,)), ((), ())), preferred_element_type=F32
+    )
+    sums = sums[0:MOMENTS] + sums[MOMENTS : 2 * MOMENTS]
+    loads[...] = jnp.zeros_like(loads)
+    loads[:, 0:ROWS] = sums[0:8]
+    loads[:, NZ : NZ + ROWS] = sums[8:16]
+    for t in BESIDE:
+        message[t, 8:16, :] = loads[...]
 
     def length(t):
         dx, dy = NEAR[t]
-        return 8 if abs(dx) == 2 else 16 if dx and dy else 72
+        return 8 if abs(dx) == 2 else 24 if dx and dy else 80
 
     pl.semaphore_wait(barrier, 14)
     near = {}
@@ -356,53 +375,27 @@
         )
         near[there].start()
 
-    def halves(chunk, carry):
-        for row in range(CX):
-            value = parts[chunk, pl.ds(row, MOMENTS, stride=CX), :]
-            high = value.astype(jnp.bfloat16).astype(F32)
-            both = jnp.concatenate([high, value - high], axis=0)
-            at = pl.multiple_of(row * CELLS + chunk * LANES, LANES)
-            split[:, pl.ds(at, LANES)] = both.astype(jnp.bfloat16)
-        return carry
-
-    lax.fori_loop(0, CHUNKS, halves, 0, unroll=8)
-    sums = lax.dot_general(
-        split[...], weights[...], (((1,), (1,)), ((), ())), preferred_element_type=F32
-    )
-    loads[...] = jnp.zeros_like(loads)
-    loads[:, 0:ROWS] = sums[0:MOMENTS] + sums[MOMENTS : 2 * MOMENTS]
-    beside = {}
-    for n, t in enumerate(BESIDE):
-        there = 14 - t
-        beside[there] = pltpu.make_async_remote_copy(
-            src_ref=loads, dst_ref=loads_in.at[there],
-            send_sem=load_send.at[n], recv_sem=load_recv.at[there],
-            device_id=device(t), device_id_type=MESH,
-        )
-        beside[there].start()
-
     for t in SENDS:
         near[t].wait()
-    group = (lanes8 - 4) >> 2
-    full = jnp.where(group == HERE, state[...], 0.0)
+    group = (lanes8 & 63) >> 2
+    full = state[...]
     for t in SENDS:
         full = jnp.where(group == t, arrived[t, 0:8, :], full)
-    place = full[0:1].astype(jnp.int32)
     group = group[0:1]
     group_x = (
         (group >= 3).astype(jnp.int32) + (group >= 6).astype(jnp.int32)
         + (group >= 9).astype(jnp.int32) + (group >= 12).astype(jnp.int32)
     )
-    table[0:1, :] = ((place & (CX - 1)) + (group_x - 2) * CX).astype(F32)
-    table[1:2, :] = ((place >> 3) + (group - 3 * group_x - 1) * CY).astype(F32)
-    table[2:9, :] = full[1:8]
+    moved = jnp.where(lane < NZ, (group_x - 2) * CX, (group - 3 * group_x - 1) * CY)
+    table[0:1, :] = full[0:1] + moved.astype(F32)
+    table[1:8, :] = full[1:8]
 
     def covers(chunk, carry):
         at = pl.ds(pl.multiple_of(chunk * LANES, LANES), LANES)
         cell_y = ((lanes8 >> 6) + 2 * chunk).astype(F32)
         terms = sphere_terms(
             post[19, :, at], [codes[layer, :, at] for layer in range(2)], table,
-            (cell_x, cell_y, cell_z), 4 + 4 * 3,
+            (cell_x, cell_y, cell_z), 12,
         )
         post[0, :, at] = post[0, :, at] + terms[0][0]
         for pop in range(1, 19):
@@ -415,14 +408,14 @@
     halo_x = {}
     for side, names in ((0, X_UP), (1, X_DOWN)):
         t = NEAR.index((-1 if side == 0 else 1, 0))
-        got = [arrived[t, 8 + 8 * n : 16 + 8 * n, :] for n in range(8)]
+        got = [arrived[t, 16 + 8 * n : 24 + 8 * n, :] for n in range(8)]
         cells = (
             jnp.full((CX, LANES), -1.0 if side == 0 else float(CX), F32),
             (2 * rows8 + (lanes8 >> 6)).astype(F32),
             cell_z,
         )
         terms = sphere_terms(
-            got[5], [v.astype(jnp.int32) for v in got[6:8]], table, cells, 16 + (-12 if side == 0 else 12)
+            got[5], [v.astype(jnp.int32) for v in got[6:8]], table, cells, 12 + (-12 if side == 0 else 12)
         )
         for n, pop in enumerate(names):
             value = got[n] + term_of(terms, pop)
@@ -435,12 +428,12 @@
                 value = jnp.where(crossed, pltpu.roll(value, step_y % CX, 0), value)
             halo_x[pop] = value
     from_low, from_high = NEAR.index((0, -1)), NEAR.index((0, 1))
-    got_low = [arrived[from_low, 8 + 8 * n : 16 + 8 * n, :] for n in range(8)]
-    got_high = [arrived[from_high, 8 + 8 * n : 16 + 8 * n, :] for n in range(8)]
+    got_low = [arrived[from_low, 16 + 8 * n : 24 + 8 * n, :] for n in range(8)]
+    got_high = [arrived[from_high, 16 + 8 * n : 24 + 8 * n, :] for n in range(8)]
     mixed = [jnp.where(lower, got_high[n], got_low[n]) for n in range(5, 8)]
     cells = (cell_x, jnp.where(lower, float(CY), -1.0), cell_z)
     terms = sphere_terms(
-        mixed[0], [v.astype(jnp.int32) for v in mixed[1:]], table, cells, jnp.where(lower, 20, 12)
+        mixed[0], [v.astype(jnp.int32) for v in mixed[1:]], table, cells, jnp.where(lower, 16, 8)
     )
     halo_y = {}
     for names, got in ((Y_UP, got_low), (Y_DOWN, got_high)):
@@ -458,11 +451,11 @@
         t = NEAR.index((sx, sy))
         here = rows8 == row
         for n in range(4):
-            piece = jnp.broadcast_to(arrived[t, 8 + n : 9 + n, :], (CX, LANES))
+            piece = jnp.broadcast_to(arrived[t, 16 + n : 17 + n, :], (CX, LANES))
             corner[n] = jnp.where(here, piece, corner[n])
         corner_x = jnp.where(here, -1.0 if sx < 0 else float(CX), corner_x)
         corner_y = jnp.where(here, -1.0 if sy < 0 else float(CY), corner_y)
-        corner_slot = jnp.where(here, 16 + 12 * sx + 4 * sy, corner_slot)
+        corner_slot = jnp.where(here, 12 + 12 * sx + 4 * sy, corner_slot)
     terms = sphere_terms(
         corner[1], [v.astype(jnp.int32) for v in corner[2:4]], table, (corner_x, corner_y, cell_z), corner_slot
     )
@@ -477,19 +470,17 @@
         halo[1, n] = halo_y[pop]
     corner_out[...] = corner_of
 
-    for t in BESIDE:
-        beside[t].wait()
-    lanes16 = lax.broadcasted_iota(jnp.int32, (MOMENTS, LANES), 1) >> 2
-    moment = jnp.where(lanes16 == 4, loads[...], 0.0)
+    named = (lanes8 & 63) >> 2
+    moment = jnp.where(named == 4, loads[...], 0.0)
     for t in BESIDE:
         dx, dy = NEAR[t]
-        moment = jnp.where(lanes16 == (1 - dx) * 3 + 1 - dy, loads_in[t], moment)
-    m = [moment[n : n + 1, :] for n in range(MOMENTS)]
+        moment = jnp.where(named == (1 - dx) * 3 + 1 - dy, arrived[t, 8:16, :], moment)
+    upper = pltpu.roll(moment, NZ, 1)
+    m = [half[n : n + 1, :] for half in (moment, upper) for n in range(8)]
     group = lane >> 2
     group_x = (group >= 3).astype(jnp.int32) + (group >= 6).astype(jnp.int32)
-    place = state[0:1, :].astype(jnp.int32)
-    cx = ((place & (CX - 1)) + (group_x - 1) * CX).astype(F32)
-    cy = ((place >> 3) + (group - 3 * group_x - 1) * CY).astype(F32)
+    cx = state[0:1, :] + ((group_x - 1) * CX).astype(F32)
+    cy = pltpu.roll(state[0:1, :], NZ, 1) + ((group - 3 * group_x - 1) * CY).astype(F32)
     cz = state[1:2, :] - 32.0
     vx, vy, vz, sx, sy, sz = [state[n : n + 1, :] for n in range(2, 8)]
     ex, ey, ez = m[1] - cx * m[0], m[2] - cy * m[0], m[3] - cz * m[0]
@@ -586,15 +577,12 @@
             pltpu.VMEM((ROWS, CX * CELLS), jnp.bfloat16),
             pltpu.VMEM((2 * MOMENTS, CX * CELLS), jnp.bfloat16),
             pltpu.VMEM((8, LANES), F32),
-            pltpu.VMEM((15, 72, LANES), F32),
-            pltpu.VMEM((15, 72, LANES), F32),
-            pltpu.VMEM((16, LANES), F32),
-            pltpu.VMEM((MOMENTS, LANES), F32),
-            pltpu.VMEM((15, MOMENTS, LANES), F32),
+            pltpu.VMEM((15, 80, LANES), F32),
+            pltpu.VMEM((15, 80, LANES), F32),
+            pltpu.VMEM((8, LANES), F32),
+            pltpu.VMEM((8, LANES), F32),
             dma((7,)),
             dma((14,)),
-            dma((15,)),
-            dma((8,)),
             dma((15,)),
         ],
         compiler_params=pltpu.CompilerParams(

time: 29.2 us -> 28.8 us (0.986)
  Pallas kernels: 28.4 us -> 28 us
    pallas_call x1, Pallas kernels: 27.4 us -> 27 us  [per_device(): pl.pallas_call(kernel, out_shape=(pltpu.VMEM((20, CX, CELLS), F32), pltpu...]
where the time goes in v5:
time: 28.8 us; the launch traced here: 28.6 us
  Pallas kernels  28 us (97%)
  between operations  0.64 us (2%)
    pallas_call x1, Pallas kernels, per_device(): pl.pallas_call(kernel, out_shape=(pltpu.VMEM((20, CX, CELLS), F32), pltpu...  27 us
    pallas_call x1, Pallas kernels, per_device(): pl.pallas_call(finish, out_shape=(jax.ShapeDtypeStruct((19, CX, CELLS), F...  1.03 us

profile of v5, /device:TPU:1, one launch (start us, length us, event | category | flops | bytes accessed | tf_op | source)
XLA Modules:
  0.0 28.6 jit_solution(3315584669474586544)
XLA Ops:
  0.6 27.0 %shard_map.86 = (f32[20,8,1024]{2,1,0:T(8,128)S(1)}, f32[2,10,8,128]{3,2,1,0:T(8,128)S(1)}, f32[8,128]{1,0:T(8,128)S(1)}, f32[4,6]{1,0:T(4,128)S(1)}) custom-call(f32[19,8,1024]{2,1,0:T(8,128)} %pops_hbm.1, s32[2,8,1024]{2,1,0:T(8,128)} %codes_hbm.1, s32[3,1,1,4]{3,2,1,0:T(1,128)} %cell_hbm.1, f32[3,1,1,4]{3,2,1,0:T(1,128)} %vel_hbm.1, ...), custom_call_target="tpu_custom_call" | custom-call | tf_op jit(solution)/shard_map/pallas_call | solution.py:557
  27.6 1.0 %shard_map.87 = (f32[19,8,1024]{2,1,0:T(8,128)}, f32[4,6]{1,0:T(4,128)}) custom-call(f32[20,8,1024]{2,1,0:T(8,128)S(1)} %get-tuple-element.8.post, f32[2,10,8,128]{3,2,1,0:T(8,128)S(1)} %get-tuple-element.9.halo, f32[8,128]{1,0:T(8,128)S(1)} %get-tuple-element.10.corner_of, f32[4,6]{1,0:T(4,128)S(1)} %get-tuple-element.11.load), custom_call_target="tpu_custom_call" | custom-call | tf_op jit(solution)/shard_map/pallas_call | solution.py:595

commit v6 on v5

--- a/solution.py
+++ b/solution.py
@@ -45,6 +45,7 @@
 HERE = NEAR.index((0, 0))
 SENDS = [0, 2, 12, 14, 3, 5, 9, 11, 1, 13, 4, 10, 6, 8]
 BESIDE = [t for t in SENDS if abs(NEAR[t][0]) < 2]
+STRAIGHT = 3
 CORNERS = {7: (-1, -1), 8: (1, 1), 9: (-1, 1), 10: (1, -1)}
 MOMENTS = 16
 ROWS = 48
@@ -102,6 +103,20 @@
     return table
 
 
+def length(t):
+    dx, dy = NEAR[t]
+    return 0 if t == HERE else 1 if abs(dx) == 2 else 12 if dx and dy else 72 if dx else 40
+
+
+FIRST = [0] + [sum(-(-length(t) // 8) * 8 for t in range(n + 1)) for n in range(15)]
+TOTAL = FIRST[15]
+SENT = sum(length(t) for t in range(15))
+
+
+def rows_of(t, start, stop):
+    return slice(FIRST[t] + start, FIRST[t] + stop)
+
+
 def lane_shift(pop):
     return int(VELOCITIES[pop, 1]) * NZ + int(VELOCITIES[pop, 2])
 
@@ -111,17 +126,16 @@
     for packed in codes:
         slot = ((packed >> 8) + first_slot) & 63
         weight = (packed & 255).astype(F32) * (1.0 / 255.0) * density
-        got = [
+        ax, ay, az, sx, sy, sz = [
             jnp.take_along_axis(
-                jnp.broadcast_to(table[n : n + 1, :], (CX, LANES)), at,
+                jnp.broadcast_to(table[n : n + 1, :], (CX, LANES)), slot,
                 axis=1, mode="promise_in_bounds",
             )
-            for n, at in ((0, slot), (0, slot + 64), *((n, slot) for n in range(1, 8)))
+            for n in range(6)
         ]
-        rx, ry, rz = cell[0] - got[0], cell[1] - got[1], cell[2] - got[2]
-        wx = got[3] + got[7] * rz - got[8] * ry
-        wy = got[4] + got[8] * rx - got[6] * rz
-        wz = got[5] + got[6] * ry - got[7] * rx
+        wx = ax + (sy * cell[2] - sz * cell[1])
+        wy = ay + (sz * cell[0] - sx * cell[2])
+        wz = az + (sx * cell[1] - sy * cell[0])
         bx, by, bz = weight * wx, weight * wy, weight * wz
         one = (bx, by, bz)
         two = (bx * wx, by * wy, bz * wz, bx * wy, bx * wz, by * wz)
@@ -167,9 +181,15 @@
     nx, ny = lax.axis_size("bx"), lax.axis_size("by")
     me_x, me_y = lax.axis_index("bx"), lax.axis_index("by")
 
+    def wrapped(at, size):
+        return jnp.where(at < 0, at + size, jnp.where(at >= size, at - size, at))
+
+    x_of = {d: wrapped(me_x + d, nx) for d in range(-2, 3)}
+    y_of = {d: wrapped(me_y + d, ny) for d in range(-1, 2)}
+
     def device(t):
         dx, dy = NEAR[t]
-        return (lax.rem(me_x + dx + nx, nx), lax.rem(me_y + dy + ny, ny))
+        return (x_of[dx], y_of[dy])
 
     barrier = pltpu.get_barrier_semaphore()
     for t in SENDS:
@@ -203,8 +223,6 @@
             rows.append(along([source[n, 0, 0, k] for k in range(4)]))
     for n, row in enumerate(rows):
         state[n : n + 1, :] = row
-    for t in SENDS:
-        message[t, 0:8, :] = state[...]
 
     which = lax.broadcasted_iota(jnp.int32, (16, LANES), 0)
     rates = jnp.zeros((16, LANES), F32)
@@ -320,7 +338,7 @@
         for row, names in ((CX - 1, X_UP), (0, X_DOWN)):
             t = NEAR.index((1 if row else -1, 0))
             for n, value in enumerate([g[pop] for pop in names] + common):
-                message[t, pl.ds(16 + 8 * n + chunk, 1), :] = value[row : row + 1, :]
+                message[pl.ds(FIRST[t] + 8 + 8 * n + chunk, 1), :] = value[row : row + 1, :]
         return carry
 
     lax.fori_loop(0, CHUNKS, fluid, 0, unroll=8)
@@ -330,15 +348,19 @@
         c = CHUNKS - 1 if dy > 0 else 0
         t = NEAR.index((0, dy))
         at = slice(c * LANES, (c + 1) * LANES)
-        for n, value in enumerate([post[pop, :, at] for pop in (*names, 19)] + codes_f[c]):
-            message[t, 16 + 8 * n : 24 + 8 * n, :] = value
+        straight = [post[19, :, at], *codes_f[c], post[names[STRAIGHT], :, at]]
+        turned = [pltpu.roll(post[pop, :, at], NZ, 1) for n, pop in enumerate(names) if n != STRAIGHT]
+        for n, (one, two) in enumerate(zip(straight, turned)):
+            message[rows_of(t, 8 + 8 * n, 16 + 8 * n), :] = jnp.where(
+                lanes8 < NZ, *((two, one) if dy > 0 else (one, two))
+            )
     for pop, (sx, sy) in CORNERS.items():
         t = NEAR.index((-sx, -sy))
         row = CX - 1 if sx < 0 else 0
         c = CHUNKS - 1 if sy < 0 else 0
         at = slice(c * LANES, (c + 1) * LANES)
         for n, value in enumerate([post[pop, :, at], post[19, :, at]] + codes_f[c]):
-            message[t, 16 + n : 17 + n, :] = value[row : row + 1, :]
+            message[rows_of(t, 8 + n, 9 + n), :] = value[row : row + 1, :]
 
     def halves(chunk, carry):
         for row in range(CX):
@@ -354,41 +376,54 @@
         split[...], weights[...], (((1,), (1,)), ((), ())), preferred_element_type=F32
     )
     sums = sums[0:MOMENTS] + sums[MOMENTS : 2 * MOMENTS]
-    loads[...] = jnp.zeros_like(loads)
+    loads[...] = state[...]
     loads[:, 0:ROWS] = sums[0:8]
     loads[:, NZ : NZ + ROWS] = sums[8:16]
     for t in BESIDE:
-        message[t, 8:16, :] = loads[...]
-
-    def length(t):
-        dx, dy = NEAR[t]
-        return 8 if abs(dx) == 2 else 24 if dx and dy else 80
+        message[rows_of(t, 0, 8), :] = loads[...]
+    packed = jnp.zeros((1, LANES), F32)
+    for n, row in enumerate((place[0], *rows[1:], place[1])):
+        packed = jnp.where(lane >> 2 == n, row, packed)
+    for t in SENDS:
+        if t not in BESIDE:
+            message[rows_of(t, 0, 1), :] = packed
 
     pl.semaphore_wait(barrier, 14)
-    near = {}
-    for n, t in enumerate(SENDS):
+    for t in SENDS:
         there = 14 - t
-        near[there] = pltpu.make_async_remote_copy(
-            src_ref=message.at[t, 0 : length(t)], dst_ref=arrived.at[there, 0 : length(t)],
-            send_sem=near_send.at[n], recv_sem=near_recv.at[there],
+        pltpu.make_async_remote_copy(
+            src_ref=message.at[rows_of(t, 0, length(t))],
+            dst_ref=arrived.at[rows_of(there, 0, length(t))],
+            send_sem=near_send.at[0], recv_sem=near_recv.at[0],
             device_id=device(t), device_id_type=MESH,
-        )
-        near[there].start()
-
-    for t in SENDS:
-        near[t].wait()
+        ).start()
+
+    pltpu.make_async_copy(arrived.at[0:SENT], arrived.at[0:SENT], near_recv.at[0]).wait()
     group = (lanes8 & 63) >> 2
     full = state[...]
+    where = jnp.where(lanes8 < NZ, ROWS, NZ + ROWS) + (lanes8 & 3)
+    afar = 4 * jnp.where(jnp.logical_and(lanes8 >= NZ, rows8 == 0), 8, rows8) + (lanes8 & 3)
     for t in SENDS:
-        full = jnp.where(group == t, arrived[t, 0:8, :], full)
+        if t in BESIDE:
+            tile, at = arrived[rows_of(t, 0, 8), :], where
+        else:
+            tile, at = jnp.broadcast_to(arrived[rows_of(t, 0, 1), :], (CX, LANES)), afar
+        spread = jnp.take_along_axis(tile, at, axis=1, mode="promise_in_bounds")
+        full = jnp.where(group == t, spread, full)
     group = group[0:1]
     group_x = (
         (group >= 3).astype(jnp.int32) + (group >= 6).astype(jnp.int32)
         + (group >= 9).astype(jnp.int32) + (group >= 12).astype(jnp.int32)
     )
     moved = jnp.where(lane < NZ, (group_x - 2) * CX, (group - 3 * group_x - 1) * CY)
-    table[0:1, :] = full[0:1] + moved.astype(F32)
-    table[1:8, :] = full[1:8]
+    centre_x = full[0:1] + moved.astype(F32)
+    centre_y = pltpu.roll(centre_x, NZ, 1)
+    centre_z = full[1:2]
+    spin_x, spin_y, spin_z = full[5:6], full[6:7], full[7:8]
+    table[0:1, :] = full[2:3] - (spin_y * centre_z - spin_z * centre_y)
+    table[1:2, :] = full[3:4] - (spin_z * centre_x - spin_x * centre_z)
+    table[2:3, :] = full[4:5] - (spin_x * centre_y - spin_y * centre_x)
+    table[3:6, :] = full[5:8]
 
     def covers(chunk, carry):
         at = pl.ds(pl.multiple_of(chunk * LANES, LANES), LANES)
@@ -408,7 +443,7 @@
     halo_x = {}
     for side, names in ((0, X_UP), (1, X_DOWN)):
         t = NEAR.index((-1 if side == 0 else 1, 0))
-        got = [arrived[t, 16 + 8 * n : 24 + 8 * n, :] for n in range(8)]
+        got = [arrived[rows_of(t, 8 + 8 * n, 16 + 8 * n), :] for n in range(8)]
         cells = (
             jnp.full((CX, LANES), -1.0 if side == 0 else float(CX), F32),
             (2 * rows8 + (lanes8 >> 6)).astype(F32),
@@ -428,9 +463,9 @@
                 value = jnp.where(crossed, pltpu.roll(value, step_y % CX, 0), value)
             halo_x[pop] = value
     from_low, from_high = NEAR.index((0, -1)), NEAR.index((0, 1))
-    got_low = [arrived[from_low, 16 + 8 * n : 24 + 8 * n, :] for n in range(8)]
-    got_high = [arrived[from_high, 16 + 8 * n : 24 + 8 * n, :] for n in range(8)]
-    mixed = [jnp.where(lower, got_high[n], got_low[n]) for n in range(5, 8)]
+    got_low = [arrived[rows_of(from_low, 8 + 8 * n, 16 + 8 * n), :] for n in range(4)]
+    got_high = [arrived[rows_of(from_high, 8 + 8 * n, 16 + 8 * n), :] for n in range(4)]
+    mixed = [jnp.where(lower, got_high[n], got_low[n]) for n in range(3)]
     cells = (cell_x, jnp.where(lower, float(CY), -1.0), cell_z)
     terms = sphere_terms(
         mixed[0], [v.astype(jnp.int32) for v in mixed[1:]], table, cells, jnp.where(lower, 16, 8)
@@ -438,8 +473,12 @@
     halo_y = {}
     for names, got in ((Y_UP, got_low), (Y_DOWN, got_high)):
         for n, pop in enumerate(names):
-            value = got[n] + term_of(terms, pop)
-            value = pltpu.roll(value, lane_shift(pop) % LANES, 1)
+            if n == STRAIGHT:
+                value = pltpu.roll(got[3] + term_of(terms, pop), lane_shift(pop) % LANES, 1)
+            else:
+                value = got[n - (n > STRAIGHT)] + pltpu.roll(term_of(terms, pop), NZ, 1)
+                if VELOCITIES[pop, 2]:
+                    value = pltpu.roll(value, int(VELOCITIES[pop, 2]) % LANES, 1)
             step_x = int(VELOCITIES[pop, 0])
             if step_x:
                 value = pltpu.roll(value, step_x % CX, 0)
@@ -451,7 +490,7 @@
         t = NEAR.index((sx, sy))
         here = rows8 == row
         for n in range(4):
-            piece = jnp.broadcast_to(arrived[t, 16 + n : 17 + n, :], (CX, LANES))
+            piece = jnp.broadcast_to(arrived[rows_of(t, 8 + n, 9 + n), :], (CX, LANES))
             corner[n] = jnp.where(here, piece, corner[n])
         corner_x = jnp.where(here, -1.0 if sx < 0 else float(CX), corner_x)
         corner_y = jnp.where(here, -1.0 if sy < 0 else float(CY), corner_y)
@@ -474,7 +513,7 @@
     moment = jnp.where(named == 4, loads[...], 0.0)
     for t in BESIDE:
         dx, dy = NEAR[t]
-        moment = jnp.where(named == (1 - dx) * 3 + 1 - dy, arrived[t, 8:16, :], moment)
+        moment = jnp.where(named == (1 - dx) * 3 + 1 - dy, arrived[rows_of(t, 0, 8), :], moment)
     upper = pltpu.roll(moment, NZ, 1)
     m = [half[n : n + 1, :] for half in (moment, upper) for n in range(8)]
     group = lane >> 2
@@ -506,6 +545,7 @@
     for g in range(1, 9):
         total = total + pltpu.roll(tile, LANES - 4 * g, 1)
     load_ref[...] = total.T[0:4, 0:6]
+    pltpu.make_async_copy(message.at[0:SENT], message.at[0:SENT], near_send.at[0]).wait()
 
 
 def finish(post, halo, corner_of, load, out_hbm, load_hbm, out, out_sem):
@@ -577,13 +617,13 @@
             pltpu.VMEM((ROWS, CX * CELLS), jnp.bfloat16),
             pltpu.VMEM((2 * MOMENTS, CX * CELLS), jnp.bfloat16),
             pltpu.VMEM((8, LANES), F32),
-            pltpu.VMEM((15, 80, LANES), F32),
-            pltpu.VMEM((15, 80, LANES), F32),
+            pltpu.VMEM((TOTAL, LANES), F32),
+            pltpu.VMEM((TOTAL, LANES), F32),
             pltpu.VMEM((8, LANES), F32),
             pltpu.VMEM((8, LANES), F32),
             dma((7,)),
-            dma((14,)),
-            dma((15,)),
+            dma((1,)),
+            dma((1,)),
         ],
         compiler_params=pltpu.CompilerParams(
             collective_id=0, has_side_effects=True, vmem_limit_bytes=60 * 1024 * 1024

time: 28.8 us -> 28.4 us (0.986)
  Pallas kernels: 28 us -> 27.6 us
    pallas_call x1, Pallas kernels: 27 us -> 26.5 us  [per_device(): pl.pallas_call(kernel, out_shape=(pltpu.VMEM((20, CX, CELLS), F32), pltpu...]
where the time goes in v6:
time: 28.4 us; the launch traced here: 28.2 us
  Pallas kernels  27.6 us (97%)
  between operations  0.64 us (2%)
    pallas_call x1, Pallas kernels, per_device(): pl.pallas_call(kernel, out_shape=(pltpu.VMEM((20, CX, CELLS), F32), pltpu...  26.5 us
    pallas_call x1, Pallas kernels, per_device(): pl.pallas_call(finish, out_shape=(jax.ShapeDtypeStruct((19, CX, CELLS), F...  1.03 us

profile of v6, /device:TPU:1, one launch (start us, length us, event | category | flops | bytes accessed | tf_op | source)
XLA Modules:
  0.0 28.2 jit_solution(7762459118995457471)
XLA Ops:
  0.6 26.5 %shard_map.86 = (f32[20,8,1024]{2,1,0:T(8,128)S(1)}, f32[2,10,8,128]{3,2,1,0:T(8,128)S(1)}, f32[8,128]{1,0:T(8,128)S(1)}, f32[4,6]{1,0:T(4,128)S(1)}) custom-call(f32[19,8,1024]{2,1,0:T(8,128)} %pops_hbm.1, s32[2,8,1024]{2,1,0:T(8,128)} %codes_hbm.1, s32[3,1,1,4]{3,2,1,0:T(1,128)} %cell_hbm.1, f32[3,1,1,4]{3,2,1,0:T(1,128)} %vel_hbm.1, ...), custom_call_target="tpu_custom_call" | custom-call | tf_op jit(solution)/shard_map/pallas_call | solution.py:597
  27.2 1.0 %shard_map.87 = (f32[19,8,1024]{2,1,0:T(8,128)}, f32[4,6]{1,0:T(4,128)}) custom-call(f32[20,8,1024]{2,1,0:T(8,128)S(1)} %get-tuple-element.8.post, f32[2,10,8,128]{3,2,1,0:T(8,128)S(1)} %get-tuple-element.9.halo, f32[8,128]{1,0:T(8,128)S(1)} %get-tuple-element.10.corner_of, f32[4,6]{1,0:T(4,128)S(1)} %get-tuple-element.11.load), custom_call_target="tpu_custom_call" | custom-call | tf_op jit(solution)/shard_map/pallas_call | solution.py:635

commit v7 on v6

--- a/solution.py
+++ b/solution.py
@@ -43,7 +43,7 @@
 Y_UP, Y_DOWN = (3, 7, 10, 15, 17), (4, 8, 9, 16, 18)
 NEAR = [(dx, dy) for dx in range(-2, 3) for dy in range(-1, 2)]
 HERE = NEAR.index((0, 0))
-SENDS = [0, 2, 12, 14, 3, 5, 9, 11, 1, 13, 4, 10, 6, 8]
+SENDS = [2, 14, 5, 11, 8, 0, 12, 3, 9, 6, 1, 13, 4, 10]
 BESIDE = [t for t in SENDS if abs(NEAR[t][0]) < 2]
 STRAIGHT = 3
 CORNERS = {7: (-1, -1), 8: (1, 1), 9: (-1, 1), 10: (1, -1)}
@@ -425,90 +425,6 @@
     table[2:3, :] = full[4:5] - (spin_x * centre_y - spin_y * centre_x)
     table[3:6, :] = full[5:8]
 
-    def covers(chunk, carry):
-        at = pl.ds(pl.multiple_of(chunk * LANES, LANES), LANES)
-        cell_y = ((lanes8 >> 6) + 2 * chunk).astype(F32)
-        terms = sphere_terms(
-            post[19, :, at], [codes[layer, :, at] for layer in range(2)], table,
-            (cell_x, cell_y, cell_z), 12,
-        )
-        post[0, :, at] = post[0, :, at] + terms[0][0]
-        for pop in range(1, 19):
-            post[pop, :, at] = post[pop, :, at] + term_of(terms, pop)
-        return carry
-
-    lax.fori_loop(0, CHUNKS, covers, 0, unroll=8)
-
-    lower = lanes8 < NZ
-    halo_x = {}
-    for side, names in ((0, X_UP), (1, X_DOWN)):
-        t = NEAR.index((-1 if side == 0 else 1, 0))
-        got = [arrived[rows_of(t, 8 + 8 * n, 16 + 8 * n), :] for n in range(8)]
-        cells = (
-            jnp.full((CX, LANES), -1.0 if side == 0 else float(CX), F32),
-            (2 * rows8 + (lanes8 >> 6)).astype(F32),
-            cell_z,
-        )
-        terms = sphere_terms(
-            got[5], [v.astype(jnp.int32) for v in got[6:8]], table, cells, 12 + (-12 if side == 0 else 12)
-        )
-        for n, pop in enumerate(names):
-            value = got[n] + term_of(terms, pop)
-            shift = lane_shift(pop) % LANES
-            if shift:
-                value = pltpu.roll(value, shift, 1)
-            step_y = int(VELOCITIES[pop, 1])
-            if step_y:
-                crossed = lower if step_y > 0 else jnp.logical_not(lower)
-                value = jnp.where(crossed, pltpu.roll(value, step_y % CX, 0), value)
-            halo_x[pop] = value
-    from_low, from_high = NEAR.index((0, -1)), NEAR.index((0, 1))
-    got_low = [arrived[rows_of(from_low, 8 + 8 * n, 16 + 8 * n), :] for n in range(4)]
-    got_high = [arrived[rows_of(from_high, 8 + 8 * n, 16 + 8 * n), :] for n in range(4)]
-    mixed = [jnp.where(lower, got_high[n], got_low[n]) for n in range(3)]
-    cells = (cell_x, jnp.where(lower, float(CY), -1.0), cell_z)
-    terms = sphere_terms(
-        mixed[0], [v.astype(jnp.int32) for v in mixed[1:]], table, cells, jnp.where(lower, 16, 8)
-    )
-    halo_y = {}
-    for names, got in ((Y_UP, got_low), (Y_DOWN, got_high)):
-        for n, pop in enumerate(names):
-            if n == STRAIGHT:
-                value = pltpu.roll(got[3] + term_of(terms, pop), lane_shift(pop) % LANES, 1)
-            else:
-                value = got[n - (n > STRAIGHT)] + pltpu.roll(term_of(terms, pop), NZ, 1)
-                if VELOCITIES[pop, 2]:
-                    value = pltpu.roll(value, int(VELOCITIES[pop, 2]) % LANES, 1)
-            step_x = int(VELOCITIES[pop, 0])
-            if step_x:
-                value = pltpu.roll(value, step_x % CX, 0)
-            halo_y[pop] = value
-    corner = [jnp.zeros((CX, LANES), F32) for _ in range(4)]
-    corner_x = corner_y = jnp.zeros((CX, LANES), F32)
-    corner_slot = jnp.zeros((CX, LANES), jnp.int32)
-    for row, (pop, (sx, sy)) in enumerate(CORNERS.items()):
-        t = NEAR.index((sx, sy))
-        here = rows8 == row
-        for n in range(4):
-            piece = jnp.broadcast_to(arrived[rows_of(t, 8 + n, 9 + n), :], (CX, LANES))
-            corner[n] = jnp.where(here, piece, corner[n])
-        corner_x = jnp.where(here, -1.0 if sx < 0 else float(CX), corner_x)
-        corner_y = jnp.where(here, -1.0 if sy < 0 else float(CY), corner_y)
-        corner_slot = jnp.where(here, 12 + 12 * sx + 4 * sy, corner_slot)
-    terms = sphere_terms(
-        corner[1], [v.astype(jnp.int32) for v in corner[2:4]], table, (corner_x, corner_y, cell_z), corner_slot
-    )
-    corner_term = jnp.zeros((CX, LANES), F32)
-    for row, pop in enumerate(CORNERS):
-        corner_term = jnp.where(rows8 == row, term_of(terms, pop), corner_term)
-    corner_of = pltpu.roll(corner[0] + corner_term, NZ, 1)
-
-    for n, pop in enumerate((*X_UP, *X_DOWN)):
-        halo[0, n] = halo_x[pop]
-    for n, pop in enumerate((*Y_UP, *Y_DOWN)):
-        halo[1, n] = halo_y[pop]
-    corner_out[...] = corner_of
-
     named = (lanes8 & 63) >> 2
     moment = jnp.where(named == 4, loads[...], 0.0)
     for t in BESIDE:
@@ -545,6 +461,90 @@
     for g in range(1, 9):
         total = total + pltpu.roll(tile, LANES - 4 * g, 1)
     load_ref[...] = total.T[0:4, 0:6]
+    lower = lanes8 < NZ
+    halo_x = {}
+    for side, names in ((0, X_UP), (1, X_DOWN)):
+        t = NEAR.index((-1 if side == 0 else 1, 0))
+        got = [arrived[rows_of(t, 8 + 8 * n, 16 + 8 * n), :] for n in range(8)]
+        cells = (
+            jnp.full((CX, LANES), -1.0 if side == 0 else float(CX), F32),
+            (2 * rows8 + (lanes8 >> 6)).astype(F32),
+            cell_z,
+        )
+        terms = sphere_terms(
+            got[5], [v.astype(jnp.int32) for v in got[6:8]], table, cells, 12 + (-12 if side == 0 else 12)
+        )
+        for n, pop in enumerate(names):
+            value = got[n] + term_of(terms, pop)
+            shift = lane_shift(pop) % LANES
+            if shift:
+                value = pltpu.roll(value, shift, 1)
+            step_y = int(VELOCITIES[pop, 1])
+            if step_y:
+                crossed = lower if step_y > 0 else jnp.logical_not(lower)
+                value = jnp.where(crossed, pltpu.roll(value, step_y % CX, 0), value)
+            halo_x[pop] = value
+    from_low, from_high = NEAR.index((0, -1)), NEAR.index((0, 1))
+    got_low = [arrived[rows_of(from_low, 8 + 8 * n, 16 + 8 * n), :] for n in range(4)]
+    got_high = [arrived[rows_of(from_high, 8 + 8 * n, 16 + 8 * n), :] for n in range(4)]
+    mixed = [jnp.where(lower, got_high[n], got_low[n]) for n in range(3)]
+    cells = (cell_x, jnp.where(lower, float(CY), -1.0), cell_z)
+    terms = sphere_terms(
+        mixed[0], [v.astype(jnp.int32) for v in mixed[1:]], table, cells, jnp.where(lower, 16, 8)
+    )
+    halo_y = {}
+    for names, got in ((Y_UP, got_low), (Y_DOWN, got_high)):
+        for n, pop in enumerate(names):
+            if n == STRAIGHT:
+                value = pltpu.roll(got[3] + term_of(terms, pop), lane_shift(pop) % LANES, 1)
+            else:
+                value = got[n - (n > STRAIGHT)] + pltpu.roll(term_of(terms, pop), NZ, 1)
+                if VELOCITIES[pop, 2]:
+                    value = pltpu.roll(value, int(VELOCITIES[pop, 2]) % LANES, 1)
+            step_x = int(VELOCITIES[pop, 0])
+            if step_x:
+                value = pltpu.roll(value, step_x % CX, 0)
+            halo_y[pop] = value
+    corner = [jnp.zeros((CX, LANES), F32) for _ in range(4)]
+    corner_x = corner_y = jnp.zeros((CX, LANES), F32)
+    corner_slot = jnp.zeros((CX, LANES), jnp.int32)
+    for row, (pop, (sx, sy)) in enumerate(CORNERS.items()):
+        t = NEAR.index((sx, sy))
+        here = rows8 == row
+        for n in range(4):
+            piece = jnp.broadcast_to(arrived[rows_of(t, 8 + n, 9 + n), :], (CX, LANES))
+            corner[n] = jnp.where(here, piece, corner[n])
+        corner_x = jnp.where(here, -1.0 if sx < 0 else float(CX), corner_x)
+        corner_y = jnp.where(here, -1.0 if sy < 0 else float(CY), corner_y)
+        corner_slot = jnp.where(here, 12 + 12 * sx + 4 * sy, corner_slot)
+    terms = sphere_terms(
+        corner[1], [v.astype(jnp.int32) for v in corner[2:4]], table, (corner_x, corner_y, cell_z), corner_slot
+    )
+    corner_term = jnp.zeros((CX, LANES), F32)
+    for row, pop in enumerate(CORNERS):
+        corner_term = jnp.where(rows8 == row, term_of(terms, pop), corner_term)
+    corner_of = pltpu.roll(corner[0] + corner_term, NZ, 1)
+
+    for n, pop in enumerate((*X_UP, *X_DOWN)):
+        halo[0, n] = halo_x[pop]
+    for n, pop in enumerate((*Y_UP, *Y_DOWN)):
+        halo[1, n] = halo_y[pop]
+    corner_out[...] = corner_of
+
+    def covers(chunk, carry):
+        at = pl.ds(pl.multiple_of(chunk * LANES, LANES), LANES)
+        cell_y = ((lanes8 >> 6) + 2 * chunk).astype(F32)
+        terms = sphere_terms(
+            post[19, :, at], [codes[layer, :, at] for layer in range(2)], table,
+            (cell_x, cell_y, cell_z), 12,
+        )
+        post[0, :, at] = post[0, :, at] + terms[0][0]
+        for pop in range(1, 19):
+            post[pop, :, at] = post[pop, :, at] + term_of(terms, pop)
+        return carry
+
+    lax.fori_loop(0, CHUNKS, covers, 0, unroll=8)
+
     pltpu.make_async_copy(message.at[0:SENT], message.at[0:SENT], near_send.at[0]).wait()
 
 

time: 28.4 us -> 28.3 us (level)
  no operation moved by 1% of the time
where the time goes in v7:
time: 28.3 us; the launch traced here: 28.1 us
  Pallas kernels  27.5 us (97%)
  between operations  0.64 us (2%)
    pallas_call x1, Pallas kernels, per_device(): pl.pallas_call(kernel, out_shape=(pltpu.VMEM((20, CX, CELLS), F32), pltpu...  26.4 us
    pallas_call x1, Pallas kernels, per_device(): pl.pallas_call(finish, out_shape=(jax.ShapeDtypeStruct((19, CX, CELLS), F...  1.03 us

profile of v7, /device:TPU:1, one launch (start us, length us, event | category | flops | bytes accessed | tf_op | source)
XLA Modules:
  0.0 28.1 jit_solution(3330391318449094366)
XLA Ops:
  0.6 26.4 %shard_map.86 = (f32[20,8,1024]{2,1,0:T(8,128)S(1)}, f32[2,10,8,128]{3,2,1,0:T(8,128)S(1)}, f32[8,128]{1,0:T(8,128)S(1)}, f32[4,6]{1,0:T(4,128)S(1)}) custom-call(f32[19,8,1024]{2,1,0:T(8,128)} %pops_hbm.1, s32[2,8,1024]{2,1,0:T(8,128)} %codes_hbm.1, s32[3,1,1,4]{3,2,1,0:T(1,128)} %cell_hbm.1, f32[3,1,1,4]{3,2,1,0:T(1,128)} %vel_hbm.1, ...), custom_call_target="tpu_custom_call" | custom-call | tf_op jit(solution)/shard_map/pallas_call | solution.py:597
  27.1 1.0 %shard_map.87 = (f32[19,8,1024]{2,1,0:T(8,128)}, f32[4,6]{1,0:T(4,128)}) custom-call(f32[20,8,1024]{2,1,0:T(8,128)S(1)} %get-tuple-element.8.post, f32[2,10,8,128]{3,2,1,0:T(8,128)S(1)} %get-tuple-element.9.halo, f32[8,128]{1,0:T(8,128)S(1)} %get-tuple-element.10.corner_of, f32[4,6]{1,0:T(4,128)S(1)} %get-tuple-element.11.load), custom_call_target="tpu_custom_call" | custom-call | tf_op jit(solution)/shard_map/pallas_call | solution.py:635

commit v8 on v6

--- a/solution.py
+++ b/solution.py
@@ -425,20 +425,6 @@
     table[2:3, :] = full[4:5] - (spin_x * centre_y - spin_y * centre_x)
     table[3:6, :] = full[5:8]
 
-    def covers(chunk, carry):
-        at = pl.ds(pl.multiple_of(chunk * LANES, LANES), LANES)
-        cell_y = ((lanes8 >> 6) + 2 * chunk).astype(F32)
-        terms = sphere_terms(
-            post[19, :, at], [codes[layer, :, at] for layer in range(2)], table,
-            (cell_x, cell_y, cell_z), 12,
-        )
-        post[0, :, at] = post[0, :, at] + terms[0][0]
-        for pop in range(1, 19):
-            post[pop, :, at] = post[pop, :, at] + term_of(terms, pop)
-        return carry
-
-    lax.fori_loop(0, CHUNKS, covers, 0, unroll=8)
-
     lower = lanes8 < NZ
     halo_x = {}
     for side, names in ((0, X_UP), (1, X_DOWN)):
@@ -508,6 +494,20 @@
     for n, pop in enumerate((*Y_UP, *Y_DOWN)):
         halo[1, n] = halo_y[pop]
     corner_out[...] = corner_of
+
+    def covers(chunk, carry):
+        at = pl.ds(pl.multiple_of(chunk * LANES, LANES), LANES)
+        cell_y = ((lanes8 >> 6) + 2 * chunk).astype(F32)
+        terms = sphere_terms(
+            post[19, :, at], [codes[layer, :, at] for layer in range(2)], table,
+            (cell_x, cell_y, cell_z), 12,
+        )
+        post[0, :, at] = post[0, :, at] + terms[0][0]
+        for pop in range(1, 19):
+            post[pop, :, at] = post[pop, :, at] + term_of(terms, pop)
+        return carry
+
+    lax.fori_loop(0, CHUNKS, covers, 0, unroll=8)
 
     named = (lanes8 & 63) >> 2
     moment = jnp.where(named == 4, loads[...], 0.0)
@@ -583,12 +583,13 @@
                 value = jnp.concatenate([value[:, :-LANES], jnp.where(lower, value[:, -LANES:], tile)], axis=1)
         if step_z:
             value = jnp.where(edge[step_z], post[OPPOSITE[pop]], value)
-        out[pop] = value
-        puts.append(pltpu.make_async_copy(out.at[pop], out_hbm.at[pop], out_sem.at[pop]))
+        if pop:
+            out[pop] = value
+        source = out if pop else post
+        puts.append(pltpu.make_async_copy(source.at[pop], out_hbm.at[pop], out_sem.at[0]))
         puts[-1].start()
     put_load.wait()
-    for put in puts:
-        put.wait()
+    pltpu.make_async_copy(out, out_hbm, out_sem.at[0]).wait()
 
 
 def per_device(populations, cover_codes, sphere_cell, sphere_velocity, sphere_spin, relax_rates):

time: 28.4 us -> 28.3 us (level)
  no operation moved by 1% of the time
where the time goes in v8:
time: 28.3 us; the launch traced here: 28.1 us
  Pallas kernels  27.5 us (97%)
  between operations  0.64 us (2%)
    pallas_call x1, Pallas kernels, per_device(): pl.pallas_call(kernel, out_shape=(pltpu.VMEM((20, CX, CELLS), F32), pltpu...  26.4 us
    pallas_call x1, Pallas kernels, per_device(): pl.pallas_call(finish, out_shape=(jax.ShapeDtypeStruct((19, CX, CELLS), F...  1.03 us

profile of v8, /device:TPU:1, one launch (start us, length us, event | category | flops | bytes accessed | tf_op | source)
XLA Modules:
  0.0 28.1 jit_solution(348783297207325515)
XLA Ops:
  0.6 26.4 %shard_map.86 = (f32[20,8,1024]{2,1,0:T(8,128)S(1)}, f32[2,10,8,128]{3,2,1,0:T(8,128)S(1)}, f32[8,128]{1,0:T(8,128)S(1)}, f32[4,6]{1,0:T(4,128)S(1)}) custom-call(f32[19,8,1024]{2,1,0:T(8,128)} %pops_hbm.1, s32[2,8,1024]{2,1,0:T(8,128)} %codes_hbm.1, s32[3,1,1,4]{3,2,1,0:T(1,128)} %cell_hbm.1, f32[3,1,1,4]{3,2,1,0:T(1,128)} %vel_hbm.1, ...), custom_call_target="tpu_custom_call" | custom-call | tf_op jit(solution)/shard_map/pallas_call | solution.py:598
  27.1 1.0 %shard_map.87 = (f32[19,8,1024]{2,1,0:T(8,128)}, f32[4,6]{1,0:T(4,128)}) custom-call(f32[20,8,1024]{2,1,0:T(8,128)S(1)} %get-tuple-element.8.post, f32[2,10,8,128]{3,2,1,0:T(8,128)S(1)} %get-tuple-element.9.halo, f32[8,128]{1,0:T(8,128)S(1)} %get-tuple-element.10.corner_of, f32[4,6]{1,0:T(4,128)S(1)} %get-tuple-element.11.load), custom_call_target="tpu_custom_call" | custom-call | tf_op jit(solution)/shard_map/pallas_call | solution.py:636

commit v9 on v8

--- a/solution.py
+++ b/solution.py
@@ -43,7 +43,7 @@
 Y_UP, Y_DOWN = (3, 7, 10, 15, 17), (4, 8, 9, 16, 18)
 NEAR = [(dx, dy) for dx in range(-2, 3) for dy in range(-1, 2)]
 HERE = NEAR.index((0, 0))
-SENDS = [0, 2, 12, 14, 3, 5, 9, 11, 1, 13, 4, 10, 6, 8]
+SENDS = [0, 2, 12, 14, 1, 13, 4, 10, 3, 5, 9, 11, 6, 8]
 BESIDE = [t for t in SENDS if abs(NEAR[t][0]) < 2]
 STRAIGHT = 3
 CORNERS = {7: (-1, -1), 8: (1, 1), 9: (-1, 1), 10: (1, -1)}

time: 28.3 us -> 28.7 us (1.014)
  Pallas kernels: 27.5 us -> 27.9 us
    pallas_call x1, Pallas kernels: 26.4 us -> 26.9 us  [per_device(): pl.pallas_call(kernel, out_shape=(pltpu.VMEM((20, CX, CELLS), F32), pltpu...]
where the time goes in v9:
time: 28.7 us; the launch traced here: 28.5 us
  Pallas kernels  27.9 us (97%)
  between operations  0.64 us (2%)
    pallas_call x1, Pallas kernels, per_device(): pl.pallas_call(kernel, out_shape=(pltpu.VMEM((20, CX, CELLS), F32), pltpu...  26.9 us
    pallas_call x1, Pallas kernels, per_device(): pl.pallas_call(finish, out_shape=(jax.ShapeDtypeStruct((19, CX, CELLS), F...  1.03 us

profile of v9, /device:TPU:1, one launch (start us, length us, event | category | flops | bytes accessed | tf_op | source)
XLA Modules:
  0.0 28.5 jit_solution(8278236544363751193)
XLA Ops:
  0.6 26.9 %shard_map.86 = (f32[20,8,1024]{2,1,0:T(8,128)S(1)}, f32[2,10,8,128]{3,2,1,0:T(8,128)S(1)}, f32[8,128]{1,0:T(8,128)S(1)}, f32[4,6]{1,0:T(4,128)S(1)}) custom-call(f32[19,8,1024]{2,1,0:T(8,128)} %pops_hbm.1, s32[2,8,1024]{2,1,0:T(8,128)} %codes_hbm.1, s32[3,1,1,4]{3,2,1,0:T(1,128)} %cell_hbm.1, f32[3,1,1,4]{3,2,1,0:T(1,128)} %vel_hbm.1, ...), custom_call_target="tpu_custom_call" | custom-call | tf_op jit(solution)/shard_map/pallas_call | solution.py:598
  27.5 1.0 %shard_map.87 = (f32[19,8,1024]{2,1,0:T(8,128)}, f32[4,6]{1,0:T(4,128)}) custom-call(f32[20,8,1024]{2,1,0:T(8,128)S(1)} %get-tuple-element.8.post, f32[2,10,8,128]{3,2,1,0:T(8,128)S(1)} %get-tuple-element.9.halo, f32[8,128]{1,0:T(8,128)S(1)} %get-tuple-element.10.corner_of, f32[4,6]{1,0:T(4,128)S(1)} %get-tuple-element.11.load), custom_call_target="tpu_custom_call" | custom-call | tf_op jit(solution)/shard_map/pallas_call | solution.py:636
